TPU v7x, 512 devices: a whole 4x8x8 slice. The times are simulated.
512 devices in a mesh: row: 16 (over x_lo, y), col: 32 (over z, x_hi, core).
Axes of the slice: x: 4 (x_hi: 2, x_lo: 2; x = x_hi * 2 + x_lo), y: 8, z: 8, core: 2. Of those that a mesh axis runs over, the one named last changes fastest.
Arguments:
- singles: float32 [4096, 384], P(('row', 'col')), may hold values from -6 to 6
- norm_gain: float32 [384], replicated, may hold values from 0.25 to 1.75
- w_query: float32 [384, 384], replicated, may hold values from -0.3125 to 0.3125
- w_key: float32 [384, 384], replicated, may hold values from -0.3125 to 0.3125
- w_value: float32 [384, 384], replicated, may hold values from -0.3125 to 0.3125
- w_gate: float32 [384, 384], replicated, may hold values from -0.3125 to 0.3125
- w_out: float32 [384, 384], replicated, may hold values from -0.3125 to 0.3125
- pair_bias: float32 [16, 4096, 4096], P(None, 'row', 'col'), may hold values from -6 to 256
Outputs:
- updated: float32 [4096, 384], P(('row', 'col'))
All inputs are finite; a program needn't handle non-finite values.
Results may differ from a plain program's by a relative error of at most 0.0003.
Values sent between devices are 32-bit elements; how exact they have to be, the bound alone decides.
No kernel may reach another device: no remote copies, remote signals or barrier semaphores. Data moves between devices by JAX's collectives and lax.ppermute only.
A program may use at most 64 MiB of HBM per device.

v0:
```python
import jax
import jax.numpy as jnp
from jax import lax
from jax.sharding import PartitionSpec as P


def broadcast(shard, axis, root):
    mine = lax.axis_index(axis) == root
    return lax.psum(jnp.where(mine, shard, jnp.zeros_like(shard)), axis)


def layer_norm(rows, gain):
    mean = jnp.mean(rows, axis=-1, keepdims=True)
    centred = rows - mean
    var = jnp.mean(centred * centred, axis=-1, keepdims=True)
    return centred * lax.rsqrt(var + 1e-05) * gain


def body(singles, norm_gain, w_query, w_key, w_value, w_gate, w_out, pair_bias):
    exact = lax.Precision.HIGHEST
    seg = singles.shape[0]
    heads, qrows, krows = pair_bias.shape
    width = singles.shape[1] // heads
    ratio = lax.axis_size("col") // lax.axis_size("row")
    col_index = lax.axis_index("col")
    root = col_index // ratio
    offset = col_index % ratio * krows
    normed = layer_norm(singles, norm_gain)
    w_pair = jnp.concatenate((w_key, w_value), axis=1)
    block = lax.all_gather(normed, "col", axis=0, tiled=True)
    portion = lax.dynamic_slice_in_dim(block, offset, krows, 0)
    keyside = broadcast(portion, "row", root)
    query = jnp.dot(block, w_query, precision=exact)
    pairs = jnp.dot(keyside, w_pair, precision=exact)
    dims = singles.shape[1]
    key = pairs[:, :dims].reshape(krows, heads, width)
    value = pairs[:, dims:].reshape(krows, heads, width)
    q_heads = query.reshape(qrows, heads, width)
    scale = 1.0 / jnp.sqrt(jnp.float32(width))
    scores = jnp.einsum("qhd,khd->hqk", q_heads, key, precision=exact) * scale + pair_bias
    local_top = jnp.max(scores, axis=-1)
    gate = jax.nn.sigmoid(jnp.dot(normed, w_gate, precision=exact))
    top = lax.pmax(local_top, "col")
    weights = jnp.exp(scores - top[:, :, None])
    totals = jnp.sum(weights, axis=-1).T
    sums = jnp.einsum("hqk,khd->qhd", weights, value, precision=exact).reshape(qrows, dims)
    own_sums, own_totals = (
        lax.psum_scatter(sums, "col", scatter_dimension=0, tiled=True),
        lax.psum_scatter(totals, "col", scatter_dimension=0, tiled=True),
    )
    attn = (own_sums.reshape(seg, heads, width) / own_totals[:, :, None]).reshape(seg, dims)
    return singles + jnp.dot(gate * attn, w_out, precision=exact)


def solution(mesh):
    return jax.shard_map(
        body,
        mesh=mesh,
        in_specs=(P(("row", "col"), None), P(), P(), P(), P(), P(), P(), P(None, "row", "col")),
        out_specs=P(("row", "col"), None),
        check_vma=False,
    )
```

profile of v0, /device:TPU:1, one launch (start us, length us, event | category | flops | bytes accessed | tf_op | source)
XLA Modules:
  0.0 597.1 jit_solution(3717214218690981840)
XLA Ops:
  6.5 0.9 reduce_sum.27
  7.4 0.9 multiply_reduce_fusion
  8.3 0.8 multiply_multiply_fusion
  9.1 50.3 %all_gather.3 = f32[256,384]{1,0:T(8,128)S(1)} all-gather(f32[8,384]{1,0:T(8,128)S(1)} %multiply_multiply_fusion), channel_id=1, replica_groups=mesh['row'=16,'col'=32] {'col'}, dimensions={0}, use_global_device_ids=true | all-gather | bytes 405504 | tf_op jit(solution)/shard_map/all_gather | solution.py:30
  59.4 0.7 dynamic-slice_select_fusion
  60.2 3.0 copy.22
  63.2 1.1 fusion.14
  64.3 115.5 %all-reduce.5.cloned.1.call-done = f32[128,384]{1,0:T(8,128)} async-done(((f32[128,384]{1,0:T(8,128)}), f32[128,384]{1,0:T(8,128)}) %all-reduce.5.cloned.1.call-update) | async-done | bytes 196624 | tf_op jit(solution)/shard_map/psum | solution.py:9
  179.9 1.8 fusion.2
  181.7 0.1 copy.21
  181.9 3.6 fusion.13
  185.4 134.7 %pmax.7 = f32[16,256]{1,0:T(8,128)S(1)} all-reduce(f32[16,256]{1,0:T(8,128)S(1)} %get-tuple-element.7), channel_id=1, replica_groups=mesh['row'=16,'col'=32] {'col'}, use_global_device_ids=true, to_apply=%region_4.5 | all-reduce | flops 4096 | bytes 32768 | tf_op jit(solution)/shard_map/pmax | solution.py:43
  320.2 0.1 copy.19
  320.3 2.1 fusion.1
  322.4 1.3 dynamic-slice
  324.4 0.3 fusion
  324.7 128.5 %all-reduce.1 = f32[256,16]{0,1:T(8,128)S(1)} all-reduce(f32[256,16]{0,1:T(8,128)S(1)} %bitcast.26), channel_id=3, replica_groups=mesh['row'=16,'col'=32] {'col'}, use_global_device_ids=true, to_apply=%region_7.8.clone | all-reduce | flops 4096 | bytes 32768
  453.4 0.1 div.34
  453.5 0.1 div.35
  453.6 133.1 %all-reduce.7.cloned.1.call-done = f32[256,384]{0,1:T(8,128)} async-done(((f32[256,384]{0,1:T(8,128)}), f32[256,384]{0,1:T(8,128)}) %all-reduce.7.cloned.1.call-update) | async-done | bytes 393232
  586.6 1.0 constant_dynamic-slice_fusion.1
  587.7 0.1 copy.25
  587.7 0.4 fusion.9
  588.2 2.1 convolution_add_fusion
  (19 shorter events, 0.3 us)
Async XLA Ops:
  6.5 56.7 %copy-start = (f32[384,384]{1,0:T(8,128)S(1)}, f32[384,384]{1,0:T(8,128)}, u32[]{:S(2)}) copy-start(f32[384,384]{1,0:T(8,128)} %param.10) | copy-start | bytes 1769476
  6.5 173.3 %all-reduce.5.cloned.1.call-start = ((), (), s32[]{:S(2)}) async-start(), calls=%async_computation | async-start | bytes 393216 | tf_op jit(solution)/shard_map/psum | solution.py:9
  60.1 119.8 %copy-start.1 = (f32[384,384]{1,0:T(8,128)S(1)}, f32[384,384]{1,0:T(8,128)}, u32[]{:S(2)}) copy-start(f32[384,384]{1,0:T(8,128)} %param.12) | copy-start | bytes 1769476
  60.1 119.8 %copy-start.2 = (f32[384,384]{1,0:T(8,128)S(1)}, f32[384,384]{1,0:T(8,128)}, u32[]{:S(2)}) copy-start(f32[384,384]{1,0:T(8,128)} %param.11) | copy-start | bytes 1769476
  60.1 526.5 %all-reduce.7.cloned.1.call-start = ((), (), s32[]{:S(2)}) async-start(), calls=%async_computation.1 | async-start | bytes 786432
  322.4 265.4 %copy-start.3 = (f32[384,384]{1,0:T(8,128)S(1)}, f32[384,384]{1,0:T(8,128)}, u32[]{:S(2)}) copy-start(f32[384,384]{1,0:T(8,128)} %param.13) | copy-start | bytes 1769476
  322.4 265.8 %copy-start.4 = (f32[8,384]{1,0:T(8,128)S(1)}, f32[8,384]{1,0:T(8,128)}, u32[]{:S(2)}) copy-start(f32[8,384]{1,0:T(8,128)} %param.8) | copy-start | bytes 36868
Sparse Core Ops, SparseCore 0:
  60.2 119.6 all-reduce.4
  322.5 264.0 all-reduce.6
where the time goes:
time: 598 us; the launch traced here: 597 us
  blocking collectives  314 us (53%)
  waiting for transfers between devices  249 us (42%)
  between operations  14.2 us (2%)
  matrix products  11.1 us (2%)
  local copies, waits for them, and re-layouts  6.08 us (1%)
    pmax x1, blocking collectives, body(): top = lax.pmax(local_top, 'col')  135 us
    unnamed x3, waiting for transfers between devices  133 us
    unnamed x1, blocking collectives  129 us
    psum x1, waiting for transfers between devices, broadcast(): return lax.psum(jnp.where(mine, shard, jnp.zeros_like(shard)), axis)  116 us
    all_gather x1, blocking collectives, body(): block = lax.all_gather(normed, 'col', axis=0, tiled=True)  50.3 us
  transfers between devices with their start and end apart: 2, of which 2 were waited for; matrix products, arithmetic and copies ran while one was open for 1% of the time, Pallas kernels for 0%

commit v1 on v0

v1 whole, which is shorter than its diff:
```python
import jax
import jax.numpy as jnp
from jax import lax
from jax.sharding import PartitionSpec as P

EXACT = lax.Precision.HIGHEST
ROW, COL, CHIPS = 16, 32, 16
SLICE = 8


def layer_norm(rows, gain):
    mean = jnp.mean(rows, axis=-1, keepdims=True)
    centred = rows - mean
    var = jnp.mean(centred * centred, axis=-1, keepdims=True)
    return centred * lax.rsqrt(var + 1e-05) * gain


def ring(a, b, n):
    return min((a - b) % n, (b - a) % n)


def holders(m):
    z, x_hi = divmod(m, 2)
    x_lo, y = divmod(m, 8)
    zs = sorted(range(8), key=lambda v: (-ring(v, z, 8), v))
    ys = sorted(range(8), key=lambda v: (ring(v, y, 8), v))
    out = [0] * CHIPS
    for z_from, y_to in zip(zs, ys):
        for x_from in range(2):
            out[2 * z_from + x_from] = (x_lo if x_from == x_hi else 1 - x_lo) * 8 + y_to
    return out


HOLDERS = [holders(m) for m in range(CHIPS)]
OVER_M = [[r * COL + 2 * m + k for m in range(CHIPS)] for r in range(ROW) for k in range(2)]
OVER_R = [[r * COL + 2 * m + k for r in HOLDERS[m]] for m in range(CHIPS) for k in range(2)]
SIBLING = [(i, i ^ 1) for i in range(ROW * COL)]


def to_column(flip):
    return [
        (m * COL + 2 * s + (k ^ flip), HOLDERS[m][s] * COL + 2 * m + k)
        for m in range(CHIPS)
        for s in range(CHIPS)
        for k in range(2)
    ]


AXES = ("row", "col")


def exchange(pieces, groups):
    return lax.all_to_all(pieces, AXES, 0, 0, tiled=True, axis_index_groups=groups)


def body(singles, norm_gain, w_query, w_key, w_value, w_gate, w_out, pair_bias):
    dims = singles.shape[1]
    heads, qrows, krows = pair_bias.shape
    width = dims // heads
    core = lax.axis_index("col") % 2
    normed = layer_norm(singles, norm_gain)

    near = lax.ppermute(normed, AXES, to_column(0))
    far = lax.ppermute(normed, AXES, to_column(1))
    halves = pair_bias.reshape(heads, CHIPS, 2, SLICE, krows)
    mine = lax.dynamic_index_in_dim(halves, core, 2, keepdims=False)
    theirs = lax.dynamic_index_in_dim(halves, 1 - core, 2, keepdims=False)
    got = lax.ppermute(theirs, AXES, SIBLING)
    q_in = exchange(jnp.broadcast_to(normed[None], (CHIPS, SLICE, dims)), OVER_M)
    piece = jnp.where(core == 0, jnp.concatenate((near, far)), jnp.concatenate((far, near)))
    k_in = exchange(jnp.broadcast_to(piece[None], (CHIPS, 2 * SLICE, dims)), OVER_R)

    first = jnp.where(core == 0, mine, got)
    second = jnp.where(core == 0, got, mine)
    bias = jnp.concatenate((first, second), axis=-1).reshape(heads, qrows // 2, 2 * krows)

    rows = q_in.reshape(qrows // 2, dims)
    keyside = k_in.reshape(2 * krows, dims)
    query = jnp.dot(rows, w_query, precision=EXACT).reshape(qrows // 2, heads, width)
    key = jnp.dot(keyside, w_key, precision=EXACT).reshape(2 * krows, heads, width)
    value = jnp.dot(keyside, w_value, precision=EXACT).reshape(2 * krows, heads, width)
    scale = 1.0 / jnp.sqrt(jnp.float32(width))
    scores = jnp.einsum("qhd,khd->hqk", query, key, precision=EXACT) * scale + bias
    top = jnp.max(scores, axis=-1)
    weights = jnp.exp(scores - top[:, :, None])
    totals = jnp.sum(weights, axis=-1)
    sums = jnp.einsum("hqk,khd->qhd", weights, value, precision=EXACT).reshape(qrows // 2, dims)
    message = jnp.concatenate((sums, totals.T, top.T), axis=1).reshape(CHIPS, SLICE, dims + 2 * heads)
    parts = exchange(message, OVER_M)
    tops = parts[:, :, dims + heads :]
    share = jnp.exp(tops - jnp.max(tops, axis=0))
    own_totals = jnp.sum(parts[:, :, dims : dims + heads] * share, axis=0)
    own_sums = jnp.sum(parts[:, :, :dims].reshape(CHIPS, SLICE, heads, width) * share[..., None], axis=0)
    attn = (own_sums / own_totals[:, :, None]).reshape(SLICE, dims)
    gate = jax.nn.sigmoid(jnp.dot(normed, w_gate, precision=EXACT))
    return singles + jnp.dot(gate * attn, w_out, precision=EXACT)


def solution(mesh):
    return jax.shard_map(
        body,
        mesh=mesh,
        in_specs=(P(("row", "col"), None), P(), P(), P(), P(), P(), P(), P(None, "row", "col")),
        out_specs=P(("row", "col"), None),
        check_vma=False,
    )
```

time: 598 us -> 87.5 us (0.15)
  the two profiles are of different devices: /device:TPU:1 before, /device:TPU:16 now
where the time goes in v1:
time: 87.5 us; the launch traced here: 86.9 us
  starting transfers between devices  36.2 us (41%)
  blocking collectives  21 us (24%)
  waiting for transfers between devices  8.72 us (10%)
  matrix products  7.88 us (9%)
  local copies, waits for them, and re-layouts  7.78 us (9%)
  other arithmetic  5 us (6%)
    all_to_all x2, starting transfers between devices, exchange(): lax.all_to_all(pieces, AXES, 0, 0, tiled=True, axis_index_groups=groups)  23.3 us
    all_to_all x1, blocking collectives, exchange(): lax.all_to_all(pieces, AXES, 0, 0, tiled=True, axis_index_groups=groups)  21 us
    ppermute x1, starting transfers between devices, body(): far = lax.ppermute(normed, AXES, to_column(1))  6.05 us
    all_to_all x2, waiting for transfers between devices, exchange(): lax.all_to_all(pieces, AXES, 0, 0, tiled=True, axis_index_groups=groups)  5.4 us
    ppermute x1, starting transfers between devices, body(): near = lax.ppermute(normed, AXES, to_column(0))  4.94 us
    ppermute x1, waiting for transfers between devices, body(): near = lax.ppermute(normed, AXES, to_column(0))  3.31 us
    squeeze x1, local copies, waits for them, and re-layouts, body(): theirs = lax.dynamic_index_in_dim(halves, 1 - core, 2, keepdims=False)  2.31 us
    dot_general x1, matrix products, body(): jnp.einsum('qhd,khd->hqk', query, key, precision=EXACT) * scale + bias  2.26 us
  transfers between devices with their start and end apart: 5, of which 2 were waited for; matrix products, arithmetic and copies ran while one was open for 7% of the time, Pallas kernels for 0%

profile of v1, /device:TPU:16, one launch (start us, length us, event | category | flops | bytes accessed | tf_op | source)
XLA Modules:
  0.0 86.9 jit_solution(15402417357495281638)
XLA Ops:
  0.0 0.9 %reduce_sum.45 = f32[8]{0:T(128)S(1)} reduce(f32[8,384]{1,0:T(8,128)} %param.8, f32[]{:T(128)} %constant.31.clone.1), dimensions={1}, to_apply=%region_0.1 | reduce | flops 3064 | bytes 12324 | tf_op jit(solution)/shard_map/reduce_sum | solution.py:12
  0.9 0.9 %multiply_reduce_fusion = f32[8]{0:T(128)S(1)} fusion(f32[8,384]{1,0:T(8,128)} %param.8, f32[8]{0:T(128)S(1)} %broadcast_multiply_fusion), kind=kLoop, calls=%fused_computation.27 | loop fusion | flops 9208 | bytes 12352 | tf_op jit(solution)/shard_map/reduce_sum | solution.py:14
  1.8 0.8 multiply_multiply_fusion
  2.6 0.7 broadcast_in_dim.5
  3.3 12.9 %all-to-all-start.1 = ((f32[16,8,384]{2,1,0:T(8,128)}), f32[16,8,384]{2,1,0:T(8,128)S(1)}, u32[]{:S(2)}, u32[]{:S(2)}) async-start(f32[16,8,384]{2,1,0:T(8,128)} %broadcast_in_dim.5), calls=%async_computation.1 | async-start | bytes 393216 | tf_op jit(solution)/shard_map/all_to_all | solution.py:53
  16.2 6.1 %collective-permute-start.1 = (f32[8,384]{1,0:T(8,128)S(1)}, f32[8,384]{1,0:T(8,128)S(1)}, u32[]{:S(2)}, u32[]{:S(2)}) collective-permute-start(f32[8,384]{1,0:T(8,128)S(1)} %multiply_multiply_fusion), channel_id=1, source_target_pairs={{1,128},{0,129},{3,384},{2,385},{5,96},{4,97},{7,352},{6,353},{9,6... | collective-permute-start | bytes 36872 | tf_op jit(solution)/shard_map/ppermute | solution.py:64
  22.3 4.9 %collective-permute-start = (f32[8,384]{1,0:T(8,128)S(1)}, f32[8,384]{1,0:T(8,128)S(1)}, u32[]{:S(2)}, u32[]{:S(2)}) collective-permute-start(f32[8,384]{1,0:T(8,128)S(1)} %multiply_multiply_fusion), channel_id=1, source_target_pairs={{0,128},{1,129},{2,384},{3,385},{4,96},{5,97},{6,352},{7,353},{8,6... | collective-permute-start | bytes 36872 | tf_op jit(solution)/shard_map/ppermute | solution.py:63
  27.2 3.3 %collective-permute-done = f32[8,384]{1,0:T(8,128)S(1)} collective-permute-done((f32[8,384]{1,0:T(8,128)S(1)}, f32[8,384]{1,0:T(8,128)S(1)}, u32[]{:S(2)}, u32[]{:S(2)}) %collective-permute-start) | collective-permute-done | bytes 12320 | tf_op jit(solution)/shard_map/ppermute | solution.py:63
  30.6 0.8 broadcast_in_dim.4
  31.3 10.5 %all-to-all-start = ((f32[16,16,384]{2,1,0:T(8,128)}), f32[16,16,384]{2,1,0:T(8,128)S(1)}, u32[]{:S(2)}, u32[]{:S(2)}) async-start(f32[16,16,384]{2,1,0:T(8,128)} %broadcast_in_dim.4), calls=%async_computation | async-start | bytes 786432 | tf_op jit(solution)/shard_map/all_to_all | solution.py:53
  41.8 2.3 %dynamic-slice_bitcast_fusion = f32[16,16,8,128]{3,2,1,0:T(8,128)} fusion(f32[16,16,2,8,128]{4,3,2,1,0:T(8,128)} %bitcast.52, s32[]{:T(128)S(6)} %select_n.43), kind=kLoop, calls=%fused_computation.15 | loop fusion | bytes 2097156 | tf_op jit(solution)/shard_map/jit(dynamic_index_in_dim)/squeeze | solution.py:67
  44.1 1.9 %collective-permute-start.2 = (f32[16,16,8,128]{3,2,1,0:T(8,128)}, f32[16,16,8,128]{3,2,1,0:T(8,128)}, u32[]{:S(2)}, u32[]{:S(2)}) collective-permute-start(f32[16,16,8,128]{3,2,1,0:T(8,128)} %dynamic-slice_bitcast_fusion), channel_id=1, source_target_pairs={{0,1},{1,0},{2,3},{3,2},{4,5},{5,4},{6,7},{7,6},{8,9},{9,8},{10,11... | collective-permute-start | bytes 3145736 | tf_op jit(solution)/shard_map/ppermute | solution.py:68
  46.5 1.3 %copy.14 = f32[384,384]{0,1:T(8,128)S(1)} copy(f32[384,384]{1,0:T(8,128)} %param.12) | data formatting | bytes 1179648 | tf_op args[4]
  47.8 0.6 fusion.10
  48.5 5.4 %all-to-all-done = f32[16,16,384]{2,1,0:T(8,128)S(1)} async-done(((f32[16,16,384]{2,1,0:T(8,128)}), f32[16,16,384]{2,1,0:T(8,128)S(1)}, u32[]{:S(2)}, u32[]{:S(2)}) %all-to-all-start) | async-done | bytes 393248 | tf_op jit(solution)/shard_map/all_to_all | solution.py:53
  53.9 0.8 fusion.15
  54.7 0.8 fusion.14
  55.5 1.4 %bitcast_select_fusion.1 = (f32[16,16,8,128]{3,2,1,0:T(8,128)S(1)}, f32[16,16,8,128]{3,2,1,0:T(8,128)S(1)}) fusion(f32[16,16,8,128]{3,2,1,0:T(8,128)} %collective-permute-done.2, f32[16,16,2,8,128]{4,3,2,1,0:T(8,128)S(1)} %bitcast.53, s32[]{:T(128)S(6)} %select_n.42, pred[]{:T(512)S(6)} %eq.4), kind=kLoop, calls=%fused_computation.13 | loop fusion | flops 524288 | bytes 4194309 | tf_op jit(solution)/shard_map/jit(_where)/select_n | solution.py:73
  56.9 2.3 %fusion.13 = (f32[16,128]{1,0:T(8,128)S(1)}, f32[16,128,256]{2,1,0:T(8,128)S(1)}) fusion(f32[16,16,8,128]{3,2,1,0:T(8,128)S(1)} %get-tuple-element.8, f32[16,16,8,128]{3,2,1,0:T(8,128)S(1)} %get-tuple-element.7, f32[128,16,24]{0,2,1:T(8,128)S(1)} %fusion.10, f32[256,16,24]{0,2,1:T(8,128)S(1)} %fusion.15), kind=kOutput, calls=%fused_computation.30 | convolution fusion | flops 153090048 | bytes 4792320 | tf_op jit(solution)/shard_map/qhd,khd->hqk/dot_general | solution.py:83
  59.2 0.6 fusion.1
  59.8 2.0 %fusion.3 = f32[128,16,24]{0,2,1:T(8,128)S(1)} fusion(f32[256,16,24]{0,2,1:T(8,128)S(1)} %fusion.14, f32[16,128,256]{2,1,0:T(8,128)S(1)} %get-tuple-element.10, f32[16,128]{1,0:T(8,128)S(1)} %get-tuple-element.9), kind=kOutput, calls=%fused_computation.5 | convolution fusion | flops 151519232 | bytes 2695168 | tf_op jit(solution)/shard_map/hqk,khd->qhd/dot_general | solution.py:87
  63.2 21.0 %all_to_all.15 = f32[16,8,416]{2,1,0:T(8,128)S(1)} all-to-all(f32[16,8,416]{2,1,0:T(8,128)S(1)} %pad_maximum_fusion), channel_id=1, replica_groups={{0,2,4,6,8,10,12,14,16,18,20,22,24,26,28,30},{1,3,5,7,9,11,13,15,17,19,..., dimensions={0} | all-to-all | bytes 425984 | tf_op jit(solution)/shard_map/all_to_all | solution.py:53
  84.9 0.5 mul.50
  85.9 1.0 %convolution_add_fusion = f32[8,384]{1,0:T(8,128)} fusion(f32[8,384]{1,0:T(8,128)S(1)} %copy-done.5, f32[8,384]{1,0:T(8,128)S(1)} %fusion.7, f32[384,384]{1,0:T(8,128)S(1)} %copy-done.4), kind=kOutput, calls=%fused_computation.6 | convolution fusion | flops 14158848 | bytes 626688 | tf_op jit(solution)/shard_map/dot_general | solution.py:96
  (32 shorter events, 2.9 us)
Async XLA Ops:
  0.0 85.4 %copy-start = (f32[384,384]{1,0:T(8,128)S(1)}, f32[384,384]{1,0:T(8,128)}, u32[]{:S(2)}) copy-start(f32[384,384]{1,0:T(8,128)} %param.13) | copy-start | bytes 1769476
  0.0 46.0 %copy-start.2 = (f32[384,384]{1,0:T(8,128)S(1)}, f32[384,384]{1,0:T(8,128)}, u32[]{:S(2)}) copy-start(f32[384,384]{1,0:T(8,128)} %param.10) | copy-start | bytes 1769476
  3.3 27.2 %all-to-all-start.1 = ((f32[16,8,384]{2,1,0:T(8,128)}), f32[16,8,384]{2,1,0:T(8,128)S(1)}, u32[]{:S(2)}, u32[]{:S(2)}) async-start(f32[16,8,384]{2,1,0:T(8,128)} %broadcast_in_dim.5), calls=%async_computation.1 | async-start | bytes 393216 | tf_op jit(solution)/shard_map/all_to_all | solution.py:53
  16.2 11.0 %collective-permute-start.1 = (f32[8,384]{1,0:T(8,128)S(1)}, f32[8,384]{1,0:T(8,128)S(1)}, u32[]{:S(2)}, u32[]{:S(2)}) collective-permute-start(f32[8,384]{1,0:T(8,128)S(1)} %multiply_multiply_fusion), channel_id=1, source_target_pairs={{1,128},{0,129},{3,384},{2,385},{5,96},{4,97},{7,352},{6,353},{9,6... | collective-permute-start | bytes 36872 | tf_op jit(solution)/shard_map/ppermute | solution.py:64
  22.3 8.3 %collective-permute-start = (f32[8,384]{1,0:T(8,128)S(1)}, f32[8,384]{1,0:T(8,128)S(1)}, u32[]{:S(2)}, u32[]{:S(2)}) collective-permute-start(f32[8,384]{1,0:T(8,128)S(1)} %multiply_multiply_fusion), channel_id=1, source_target_pairs={{0,128},{1,129},{2,384},{3,385},{4,96},{5,97},{6,352},{7,353},{8,6... | collective-permute-start | bytes 36872 | tf_op jit(solution)/shard_map/ppermute | solution.py:63
  31.3 14.9 %copy-start.3 = (f32[384,384]{1,0:T(8,128)S(1)}, f32[384,384]{1,0:T(8,128)}, u32[]{:S(2)}) copy-start(f32[384,384]{1,0:T(8,128)} %param.11) | copy-start | bytes 1769476
  31.3 22.5 %all-to-all-start = ((f32[16,16,384]{2,1,0:T(8,128)}), f32[16,16,384]{2,1,0:T(8,128)S(1)}, u32[]{:S(2)}, u32[]{:S(2)}) async-start(f32[16,16,384]{2,1,0:T(8,128)} %broadcast_in_dim.4), calls=%async_computation | async-start | bytes 786432 | tf_op jit(solution)/shard_map/all_to_all | solution.py:53
  44.1 11.4 %collective-permute-start.2 = (f32[16,16,8,128]{3,2,1,0:T(8,128)}, f32[16,16,8,128]{3,2,1,0:T(8,128)}, u32[]{:S(2)}, u32[]{:S(2)}) collective-permute-start(f32[16,16,8,128]{3,2,1,0:T(8,128)} %dynamic-slice_bitcast_fusion), channel_id=1, source_target_pairs={{0,1},{1,0},{2,3},{3,2},{4,5},{5,4},{6,7},{7,6},{8,9},{9,8},{10,11... | collective-permute-start | bytes 3145736 | tf_op jit(solution)/shard_map/ppermute | solution.py:68
  53.9 1.6 %copy-start.1 = (f32[16,256,128]{2,1,0:T(8,128)S(1)}, f32[16,256,128]{2,1,0:T(8,128)}, u32[]{:S(2)}) copy-start(f32[16,256,128]{2,1,0:T(8,128)} %param.15) | copy-start | bytes 6291460
  63.1 22.7 %copy-start.4 = (f32[384,384]{1,0:T(8,128)S(1)}, f32[384,384]{1,0:T(8,128)}, u32[]{:S(2)}) copy-start(f32[384,384]{1,0:T(8,128)} %param.14) | copy-start | bytes 1769476
  63.1 22.7 %copy-start.5 = (f32[8,384]{1,0:T(8,128)S(1)}, f32[8,384]{1,0:T(8,128)}, u32[]{:S(2)}) copy-start(f32[8,384]{1,0:T(8,128)} %param.8) | copy-start | bytes 36868

commit v2 on v1

v2 whole, which is shorter than its diff:
```python
import jax
import jax.numpy as jnp
from jax import lax
from jax.experimental import pallas as pl
from jax.experimental.pallas import tpu as pltpu
from jax.sharding import PartitionSpec as P

ROW, COL, CHIPS = 16, 32, 16
SLICE = 8
D, HEADS, WIDTH = 384, 16, 24
TOKENS = 256
SLOT = 32
PAD = HEADS * SLOT
GROUP = 4
GROUPS = HEADS // GROUP
LANES = 128
TOTAL, TOP = WIDTH, WIDTH + 1
F32, BF16 = jnp.float32, jnp.bfloat16


def ring(a, b, n):
    return min((a - b) % n, (b - a) % n)


def holders(m):
    z, x_hi = divmod(m, 2)
    x_lo, y = divmod(m, 8)
    zs = sorted(range(8), key=lambda v: (-ring(v, z, 8), v))
    ys = sorted(range(8), key=lambda v: (ring(v, y, 8), v))
    out = [0] * CHIPS
    for z_from, y_to in zip(zs, ys):
        for x_from in range(2):
            out[2 * z_from + x_from] = (x_lo if x_from == x_hi else 1 - x_lo) * 8 + y_to
    return out


HOLDERS = [holders(m) for m in range(CHIPS)]
OVER_M = [[r * COL + 2 * m + k for m in range(CHIPS)] for r in range(ROW) for k in range(2)]
SIBLING = [(i, i ^ 1) for i in range(ROW * COL)]


MIXED = [[r * COL + 2 * m for m in range(CHIPS)] for r in range(ROW)] + [
    [r * COL + 2 * m + 1 for r in HOLDERS[m]] for m in range(CHIPS)
]
TO_COLUMN = [(m * COL + 2 * s, HOLDERS[m][s] * COL + 2 * m + 1) for m in range(CHIPS) for s in range(CHIPS)]


AXES = ("row", "col")


def exchange(pieces, groups):
    return lax.all_to_all(pieces, AXES, 0, 0, tiled=True, axis_index_groups=groups)


def layer_norm(rows, gain):
    mean = jnp.mean(rows, axis=-1, keepdims=True)
    centred = rows - mean
    var = jnp.mean(centred * centred, axis=-1, keepdims=True)
    return centred * lax.rsqrt(var + 1e-05) * gain


def split(array):
    high = array.astype(BF16)
    return high, (array - high.astype(F32)).astype(BF16)


def dot(a, b):
    return lax.dot_general(a, b, (((1,), (0,)), ((), ())), preferred_element_type=F32)


def dot_t(a, b):
    return lax.dot_general(a, b, (((1,), (1,)), ((), ())), preferred_element_type=F32)


def dot3(a, b):
    return dot(a[0], b[0]) + (dot(a[1], b[0]) + dot(a[0], b[1]))


def iota(shape, dim):
    return lax.broadcasted_iota(jnp.int32, shape, dim)


def spread():
    feature, column = iota((D, PAD), 0), iota((D, PAD), 1)
    head = lax.shift_right_logical(feature * 2731, 16)
    return jnp.where(feature + (SLOT - WIDTH) * head == column, 1.0, 0.0).astype(BF16)


def prepare_kernel(
    core_ref, pair, gain, w_query, w_key, w_value, w_gate, w_out, bias,
    wq_h, wq_l, wkv_h, wkv_l, wo_h, wo_l, gate, gain_out, theirs, held, gain_in, sems,
):
    core = core_ref[0]
    sources = (w_query, w_key, w_value, w_gate, w_out)
    copies = [pltpu.make_async_copy(source, held.at[i], sems.at[i]) for i, source in enumerate(sources)]
    for copy in copies:
        copy.start()
    send = pltpu.make_async_copy(bias.at[:, :, 1 - core], theirs, sems.at[len(sources)])
    send.start()
    fetch = pltpu.make_async_copy(gain, gain_in, sems.at[len(sources) + 1])
    fetch.start()
    place = spread()
    fetch.wait()
    gain_rows = jnp.broadcast_to(gain_in[...], (SLICE, D))
    gain_out[...] = gain_rows
    normed = split(layer_norm(pair[pl.ds(core, 1)].reshape(SLICE, D), gain_rows))
    for i, is_query, first in ((0, True, 0), (1, False, 0), (2, False, 1)):
        copies[i].wait()
        for part, out in zip(split(held[i]), (wq_h, wq_l) if is_query else (wkv_h, wkv_l)):
            wide = dot(part, place).astype(BF16)
            if is_query:
                out[...] = wide
                continue
            for g in range(GROUPS):
                at = (2 * g + first) * LANES
                out[:, at : at + LANES] = wide[:, g * LANES : (g + 1) * LANES]
    copies[3].wait()
    opened = jax.nn.sigmoid(dot3(normed, split(held[3])))
    high = opened.astype(BF16)
    rest = opened - high.astype(F32)
    mid, low = split(rest)
    gate[...] = dot(high, place) + (dot(mid, place) + dot(low, place))
    copies[4].wait()
    out_h, out_l = split(held[4])
    for out, part in ((wo_h, out_h), (wo_l, out_l)):
        out[...] = jnp.zeros((PAD, D), BF16)
        for h in range(HEADS):
            out[SLOT * h : SLOT * h + WIDTH, :] = part[WIDTH * h : WIDTH * (h + 1), :]
    send.wait()


def in_hbm(*arrays):
    return [pltpu.with_memory_space_constraint(array, pltpu.HBM) for array in arrays]


def prepare(core, pair, gain, weights, bias):
    vmem, hbm = pl.BlockSpec(memory_space=pltpu.VMEM), pl.BlockSpec(memory_space=pl.ANY)
    shapes = [(D, PAD)] * 2 + [(D, 2 * PAD)] * 2 + [(PAD, D)] * 2
    tiles = (HEADS, CHIPS, 2, SLICE, LANES)
    return pl.pallas_call(
        prepare_kernel,
        out_shape=[pltpu.VMEM(s, BF16) for s in shapes]
        + [pltpu.VMEM((SLICE, PAD), F32), pltpu.VMEM((SLICE, D), F32), pltpu.VMEM((HEADS, CHIPS, SLICE, LANES), F32)],
        in_specs=[pl.BlockSpec(memory_space=pltpu.SMEM)] + [vmem] + [hbm] * 7,
        out_specs=[vmem] * 9,
        scratch_shapes=[pltpu.VMEM((5, D, D), F32), pltpu.VMEM((1, D), F32), pltpu.SemaphoreType.DMA((7,))],
        compiler_params=pltpu.CompilerParams(vmem_limit_bytes=20 << 20),
        cost_estimate=pl.CostEstimate(flops=2 * 2304 * D * PAD, bytes_accessed=8 << 20, transcendentals=SLICE * D),
        name="prepare",
    )(core.reshape(1), pair.reshape(2, SLICE, D), *in_hbm(gain.reshape(1, D), *weights, bias.reshape(tiles)))


def attend_kernel(core_ref, block, swapped, gain, wq_h, wq_l, wkv_h, wkv_l, bias, other, out, held, sems):
    core = core_ref[0]
    copies = []
    for g in range(GROUPS):
        heads = pl.ds(g * GROUP, GROUP)
        pair = [
            pltpu.make_async_copy(source, held.at[at, heads], sems.at[g, i])
            for i, (source, at) in enumerate(((bias.at[heads, :, core], core), (other.at[heads], 1 - core)))
        ]
        for copy in pair:
            copy.start()
        copies.append(pair)
    first = core == 0
    own, given = block[...], swapped[...]
    q_rows = jnp.where(first, block[:, pl.ds(core, 1)], swapped[:, pl.ds(core, 1)]).reshape(TOKENS // 2, D)
    k_rows = jnp.where(first, given, own).reshape(TOKENS, D)
    q_norm = split(layer_norm(q_rows, gain[:1]))
    k_norm = split(layer_norm(k_rows, gain[:1]))
    half = TOKENS // 2
    slot = lax.shift_right_logical(iota((half, LANES), 1), 5)
    within = iota((half, LANES), 1) & (SLOT - 1)
    ones = jnp.where((iota((TOKENS, LANES), 1) & (SLOT - 1)) == TOTAL, 1.0, 0.0).astype(F32)
    scale = 1.0 / WIDTH**0.5
    for g in range(GROUPS):
        cols = slice(g * LANES, (g + 1) * LANES)
        query = dot3(q_norm, (wq_h[:, cols], wq_l[:, cols])) * scale
        cols = slice(2 * g * LANES, 2 * (g + 1) * LANES)
        pairs = dot3(k_norm, (wkv_h[:, cols], wkv_l[:, cols]))
        key_h, key_l = split(pairs[:, :LANES])
        value_h, value_l = split(pairs[:, LANES:] + ones)
        query_h, query_l = split(query)
        zero = jnp.zeros_like(query_h)
        lhs_h = jnp.concatenate([jnp.where(slot == p, query_h, zero) for p in range(GROUP)])
        lhs_l = jnp.concatenate([jnp.where(slot == p, query_l, zero) for p in range(GROUP)])
        scores = dot_t(jnp.concatenate((lhs_h, lhs_l), 1), jnp.concatenate((key_h, key_h), 1)) + dot_t(lhs_h, key_l)
        for copy in copies[g]:
            copy.wait()
        tops, parts_h, parts_l = [], [], []
        for p in range(GROUP):
            h = g * GROUP + p
            added = jnp.concatenate([held[k, h].reshape(half, LANES) for k in range(2)], 1)
            one = scores[p * half : (p + 1) * half] + added
            top = jnp.max(one, axis=-1, keepdims=True)
            part_h, part_l = split(jnp.exp(one - top))
            tops.append(top)
            parts_h.append(part_h)
            parts_l.append(part_l)
        sums = dot(jnp.concatenate(parts_h), jnp.concatenate((value_h, value_l), 1))
        sums = sums[:, :LANES] + (sums[:, LANES:] + dot(jnp.concatenate(parts_l), value_h))
        tile = jnp.zeros((half, LANES), F32)
        for p in range(GROUP):
            one = jnp.where(within == TOP, tops[p], sums[p * half : (p + 1) * half])
            tile = jnp.where(slot == p, one, tile)
        out[:, :, g * LANES : (g + 1) * LANES] = tile.reshape(CHIPS, SLICE, LANES)


def attend(core, block, swapped, gain, weights, bias, other):
    vmem, hbm = pl.BlockSpec(memory_space=pltpu.VMEM), pl.BlockSpec(memory_space=pl.ANY)
    shape = (CHIPS, 2, SLICE, D)
    tiles = (HEADS, CHIPS, 2, SLICE, LANES)
    return pl.pallas_call(
        attend_kernel,
        out_shape=jax.ShapeDtypeStruct((CHIPS, SLICE, PAD), F32),
        in_specs=[pl.BlockSpec(memory_space=pltpu.SMEM)] + [vmem] * 7 + [hbm] * 2,
        out_specs=vmem,
        scratch_shapes=[pltpu.VMEM((2, HEADS, CHIPS, SLICE, LANES), F32), pltpu.SemaphoreType.DMA((GROUPS, 2))],
        compiler_params=pltpu.CompilerParams(vmem_limit_bytes=14 << 20),
        cost_estimate=pl.CostEstimate(flops=10**9, bytes_accessed=6 << 20, transcendentals=HEADS * 2**15),
        name="attend",
    )(core.reshape(1), block.reshape(shape), swapped.reshape(shape), gain, *weights, *in_hbm(bias.reshape(tiles), other))


def finish_kernel(parts, gate, wo_h, wo_l, singles, out):
    lane = iota((CHIPS * SLICE, LANES), 1)
    tops_at = lane - (lane & (SLOT - 1)) + TOP
    totals_at = tops_at[:SLICE] - TOP + TOTAL
    gated = []
    for g in range(GROUPS):
        cols = slice(g * LANES, (g + 1) * LANES)
        part = parts[:, :, cols]
        tops = jnp.take_along_axis(part.reshape(CHIPS * SLICE, LANES), tops_at, axis=1).reshape(CHIPS, SLICE, LANES)
        share = jnp.exp(tops - jnp.max(tops, axis=0, keepdims=True))
        sums = jnp.sum(part * share, axis=0)
        totals = jnp.take_along_axis(sums, totals_at, axis=1)
        gated.append(sums / totals * gate[:, cols])
    out[...] = singles[...] + dot3(split(jnp.concatenate(gated, 1)), (wo_h[...], wo_l[...]))


def finish(*args):
    return pl.pallas_call(
        finish_kernel,
        out_shape=jax.ShapeDtypeStruct((SLICE, D), F32),
        compiler_params=pltpu.CompilerParams(vmem_limit_bytes=4 << 20),
        cost_estimate=pl.CostEstimate(flops=6 * SLICE * PAD * D, bytes_accessed=2 << 20, transcendentals=CHIPS * SLICE * PAD),
        name="finish",
    )(*args)


def body(singles, norm_gain, w_query, w_key, w_value, w_gate, w_out, pair_bias):
    core = lax.axis_index("col") % 2
    beside = lax.ppermute(singles, AXES, SIBLING)
    pair = jnp.where(core == 0, jnp.concatenate((singles, beside)), jnp.concatenate((beside, singles)))
    moved = lax.ppermute(pair, AXES, TO_COLUMN)
    *ready, gain, theirs = prepare(core, pair, norm_gain, (w_query, w_key, w_value, w_gate, w_out), pair_bias)
    other = lax.ppermute(theirs, AXES, SIBLING)
    moved, *ready = lax.optimization_barrier((moved, *ready))
    gate = ready[-1]
    piece = jnp.where(core == 0, pair, moved)
    block = exchange(jnp.broadcast_to(piece[None], (CHIPS, 2 * SLICE, D)), MIXED)
    swapped = lax.ppermute(block, AXES, SIBLING)
    message = attend(core, block, swapped, gain, ready[:4], pair_bias, other)
    parts = exchange(message, OVER_M)
    return finish(parts, gate, *ready[4:6], singles)


def solution(mesh):
    return jax.shard_map(
        body,
        mesh=mesh,
        in_specs=(P(("row", "col"), None), P(), P(), P(), P(), P(), P(), P(None, "row", "col")),
        out_specs=P(("row", "col"), None),
        check_vma=False,
    )
```

time: 87.5 us -> 72.2 us (0.83)
  the two profiles are of different devices: /device:TPU:16 before, /device:TPU:2 now
where the time goes in v2:
time: 72.2 us; the launch traced here: 71.7 us
  starting transfers between devices  25.3 us (35%)
  blocking collectives  17.2 us (24%)
  waiting for transfers between devices  13.3 us (18%)
  Pallas kernels  10.8 us (15%)
  local copies, waits for them, and re-layouts  4.29 us (6%)
  other arithmetic  0.79 us (1%)
    all_to_all x1, blocking collectives, exchange(): lax.all_to_all(pieces, AXES, 0, 0, tiled=True, axis_index_groups=groups)  17.2 us
    all_to_all x1, waiting for transfers between devices, exchange(): lax.all_to_all(pieces, AXES, 0, 0, tiled=True, axis_index_groups=groups)  11.5 us
    ppermute x1, starting transfers between devices, body(): moved = lax.ppermute(pair, AXES, TO_COLUMN)  10.9 us
    all_to_all x1, starting transfers between devices, exchange(): lax.all_to_all(pieces, AXES, 0, 0, tiled=True, axis_index_groups=groups)  8.67 us
    pallas_call x1, Pallas kernels, attend(): pl.pallas_call(attend_kernel, out_shape=jax.ShapeDtypeStruct((CHIPS, SLIC...  5.22 us
    pallas_call x1, Pallas kernels, prepare(): pl.pallas_call(prepare_kernel, out_shape=[pltpu.VMEM(s, BF16) for s in sh...  4.5 us
    unnamed x8, local copies, waits for them, and re-layouts  2.27 us
    ppermute x1, starting transfers between devices, body(): other = lax.ppermute(theirs, AXES, SIBLING)  1.92 us
  transfers between devices with their start and end apart: 5, of which 3 were waited for; matrix products, arithmetic and copies ran while one was open for 2% of the time, Pallas kernels for 6%

profile of v2, /device:TPU:2, one launch (start us, length us, event | category | flops | bytes accessed | tf_op | source)
XLA Modules:
  0.0 71.7 jit_solution(15324321588573590321)
XLA Ops:
  0.0 1.9 %collective-permute-start = (f32[8,384]{1,0:T(8,128)}, f32[8,384]{1,0:T(8,128)S(1)}, u32[]{:S(2)}, u32[]{:S(2)}) collective-permute-start(f32[8,384]{1,0:T(8,128)} %singles.1), channel_id=1, source_target_pairs={{0,1},{1,0},{2,3},{3,2},{4,5},{5,4},{6,7},{7,6},{8,9},{9,8},{10,11... | collective-permute-start | bytes 36872 | tf_op jit(solution)/shard_map/ppermute | solution.py:253
  1.9 1.2 %reshape.24.gain = f32[1,384]{1,0:T(1,128)} reshape(f32[384]{0:T(512)} %param.9) | data formatting | bytes 3072 | tf_op jit(solution)/shard_map/reshape | solution.py:150
  3.2 0.1 collective-permute-done
  3.3 0.8 %maximum_select_fusion = f32[16,384]{1,0:T(8,128)S(1)} fusion(f32[8,384]{1,0:T(8,128)S(1)} %collective-permute-done, f32[8,384]{1,0:T(8,128)} %singles.1, pred[]{:T(512)S(6)} %eq.6), kind=kLoop, calls=%fused_computation | loop fusion | flops 18432 | bytes 49153 | tf_op jit(solution)/shard_map/jit(_where)/select_n | solution.py:254
  4.1 10.9 %collective-permute-start.1 = (f32[16,384]{1,0:T(8,128)S(1)}, f32[16,384]{1,0:T(8,128)S(1)}, u32[]{:S(2)}, u32[]{:S(2)}) collective-permute-start(f32[16,384]{1,0:T(8,128)S(1)} %maximum_select_fusion), channel_id=1, source_target_pairs={{0,129},{2,385},{4,97},{6,353},{8,65},{10,321},{12,33},{14,289},{1... | collective-permute-start | bytes 73736 | tf_op jit(solution)/shard_map/ppermute | solution.py:255
  15.0 4.5 %prepare.1 = (bf16[384,512]{1,0:T(8,128)(2,1)S(1)}, bf16[384,512]{1,0:T(8,128)(2,1)S(1)}, bf16[384,1024]{1,0:T(8,128)(2,1)S(1)}, bf16[384,1024]{1,0:T(8,128)(2,1...) custom-call(s32[1]{0:T(128)} %bitcast.core_ref, ...), custom_call_target="tpu_custom_call" | custom-call | flops 905969664 | bytes 8388608 | tf_op jit(solution)/shard_map/prepare/pallas_call | solution.py:140
  19.5 0.0 copy-start.3
  19.5 1.0 %copy-done.3 = f32[16,16,8,128]{3,2,1,0:T(8,128)} copy-done((f32[16,16,8,128]{3,2,1,0:T(8,128)}, f32[16,16,8,128]{3,2,1,0:T(8,128)S(1)}, u32[]{:S(2)}) %copy-start.3) | copy-done | bytes 1048600
  20.5 0.0 collective-permute-done.1
  20.5 0.6 copy-done.1
  21.1 0.8 %broadcast_in_dim.2 = f32[16,16,384]{2,1,0:T(8,128)} broadcast(f32[16,384]{1,0:T(8,128)S(1)} %broadcast_select_fusion), dimensions={1,2} | broadcast | bytes 417792 | tf_op jit(solution)/shard_map/broadcast_in_dim | solution.py:261
  21.8 8.7 %all-to-all-start = ((f32[16,16,384]{2,1,0:T(8,128)}), f32[16,16,384]{2,1,0:T(8,128)S(1)}, u32[]{:S(2)}, u32[]{:S(2)}) async-start(f32[16,16,384]{2,1,0:T(8,128)} %broadcast_in_dim.2), calls=%async_computation | async-start | bytes 786432 | tf_op jit(solution)/shard_map/all_to_all | solution.py:52
  30.5 1.9 %collective-permute-start.3 = (f32[16,16,8,128]{3,2,1,0:T(8,128)}, f32[16,16,8,128]{3,2,1,0:T(8,128)}, u32[]{:S(2)}, u32[]{:S(2)}) collective-permute-start(f32[16,16,8,128]{3,2,1,0:T(8,128)} %copy-done.3), channel_id=1, source_target_pairs={{0,1},{1,0},{2,3},{3,2},{4,5},{5,4},{6,7},{7,6},{8,9},{9,8},{10,11... | collective-permute-start | bytes 3145736 | tf_op jit(solution)/shard_map/ppermute | solution.py:257
  32.4 11.5 %all-to-all-done = f32[16,16,384]{2,1,0:T(8,128)S(1)} async-done(((f32[16,16,384]{2,1,0:T(8,128)}), f32[16,16,384]{2,1,0:T(8,128)S(1)}, u32[]{:S(2)}, u32[]{:S(2)}) %all-to-all-start) | async-done | bytes 393248 | tf_op jit(solution)/shard_map/all_to_all | solution.py:52
  43.9 1.9 %collective-permute-start.2 = (f32[16,16,384]{2,1,0:T(8,128)S(1)}, f32[16,16,384]{2,1,0:T(8,128)S(1)}, u32[]{:S(2)}, u32[]{:S(2)}) collective-permute-start(f32[16,16,384]{2,1,0:T(8,128)S(1)} %all-to-all-done), channel_id=1, source_target_pairs={{0,1},{1,0},{2,3},{3,2},{4,5},{5,4},{6,7},{7,6},{8,9},{9,8},{10,11... | collective-permute-start | bytes 1179656 | tf_op jit(solution)/shard_map/ppermute | solution.py:262
  45.8 0.0 collective-permute-done.3.other
  45.8 1.7 %collective-permute-done.2 = f32[16,16,384]{2,1,0:T(8,128)S(1)} collective-permute-done((f32[16,16,384]{2,1,0:T(8,128)S(1)}, f32[16,16,384]{2,1,0:T(8,128)S(1)}, u32[]{:S(2)}, u32[]{:S(2)}) %collective-permute-start.2) | collective-permute-done | bytes 393248 | tf_op jit(solution)/shard_map/ppermute | solution.py:262
  47.5 0.0 copy-start.2
  47.5 0.7 copy-done.2
  48.2 0.0 copy-start
  48.2 5.2 %attend.1 = f32[16,8,512]{2,1,0:T(8,128)S(1)} custom-call(s32[1]{0:T(128)} %bitcast.core_ref, f32[16,2,8,384]{3,2,1,0:T(8,128)S(1)} %bitcast.5, f32[16,2,8,384]{3,2,1,0:T(8,128)S(1)} %bitcast.6, f32[8,384]{1,0:T(8,128)S(1)} %copy-done.2, bf16[384,512]{1,0:T(8,128)(2,1)S(1)} %get-tuple-element.31.wq_h, bf16[384,512]{1,0:T(8,128)(2,1)S(1)} %get-tuple-element.32.wq_l, ...), custom_call_target="tpu_custom_call" | custom-call | flops 1000000000 | bytes 6291456 | tf_op jit(solution)/shard_map/attend/pallas_call | solution.py:213
  53.5 17.2 %all_to_all.10.parts = f32[16,8,512]{2,1,0:T(8,128)S(1)} all-to-all(f32[16,8,512]{2,1,0:T(8,128)S(1)} %attend.1), channel_id=1, replica_groups={{0,2,4,6,8,10,12,14,16,18,20,22,24,26,28,30},{1,3,5,7,9,11,13,15,17,19,..., dimensions={0} | all-to-all | bytes 524288 | tf_op jit(solution)/shard_map/all_to_all | solution.py:52
  70.6 0.0 copy-done
  70.6 1.1 %finish.1 = f32[8,384]{1,0:T(8,128)} custom-call(f32[16,8,512]{2,1,0:T(8,128)S(1)} %all_to_all.10.parts, f32[8,512]{1,0:T(8,128)S(1)} %get-tuple-element.36.gate, bf16[512,384]{1,0:T(8,128)(2,1)S(1)} %get-tuple-element.37.wo_h, bf16[512,384]{1,0:T(8,128)(2,1)S(1)} %get-tuple-element.38.wo_l, f32[8,384]{1,0:T(8,128)S(1)} %copy-done), custom_call_target="tpu_custom_call" | custom-call | flops 9437184 | bytes 2097152 | tf_op jit(solution)/shard_map/finish/pallas_call | solution.py:242
  (2 shorter events, 0.0 us)
Async XLA Ops:
  0.0 3.3 %collective-permute-start = (f32[8,384]{1,0:T(8,128)}, f32[8,384]{1,0:T(8,128)S(1)}, u32[]{:S(2)}, u32[]{:S(2)}) collective-permute-start(f32[8,384]{1,0:T(8,128)} %singles.1), channel_id=1, source_target_pairs={{0,1},{1,0},{2,3},{3,2},{4,5},{5,4},{6,7},{7,6},{8,9},{9,8},{10,11... | collective-permute-start | bytes 36872 | tf_op jit(solution)/shard_map/ppermute | solution.py:253
  4.1 16.4 %collective-permute-start.1 = (f32[16,384]{1,0:T(8,128)S(1)}, f32[16,384]{1,0:T(8,128)S(1)}, u32[]{:S(2)}, u32[]{:S(2)}) collective-permute-start(f32[16,384]{1,0:T(8,128)S(1)} %maximum_select_fusion), channel_id=1, source_target_pairs={{0,129},{2,385},{4,97},{6,353},{8,65},{10,321},{12,33},{14,289},{1... | collective-permute-start | bytes 73736 | tf_op jit(solution)/shard_map/ppermute | solution.py:255
  19.5 1.0 %copy-start.3 = (f32[16,16,8,128]{3,2,1,0:T(8,128)}, f32[16,16,8,128]{3,2,1,0:T(8,128)S(1)}, u32[]{:S(2)}) copy-start(f32[16,16,8,128]{3,2,1,0:T(8,128)S(1)} %get-tuple-element.35) | copy-start | bytes 3145732
  20.5 0.6 copy-start.1
  21.8 22.1 %all-to-all-start = ((f32[16,16,384]{2,1,0:T(8,128)}), f32[16,16,384]{2,1,0:T(8,128)S(1)}, u32[]{:S(2)}, u32[]{:S(2)}) async-start(f32[16,16,384]{2,1,0:T(8,128)} %broadcast_in_dim.2), calls=%async_computation | async-start | bytes 786432 | tf_op jit(solution)/shard_map/all_to_all | solution.py:52
  30.5 15.3 %collective-permute-start.3 = (f32[16,16,8,128]{3,2,1,0:T(8,128)}, f32[16,16,8,128]{3,2,1,0:T(8,128)}, u32[]{:S(2)}, u32[]{:S(2)}) collective-permute-start(f32[16,16,8,128]{3,2,1,0:T(8,128)} %copy-done.3), channel_id=1, source_target_pairs={{0,1},{1,0},{2,3},{3,2},{4,5},{5,4},{6,7},{7,6},{8,9},{9,8},{10,11... | collective-permute-start | bytes 3145736 | tf_op jit(solution)/shard_map/ppermute | solution.py:257
  43.9 3.6 %collective-permute-start.2 = (f32[16,16,384]{2,1,0:T(8,128)S(1)}, f32[16,16,384]{2,1,0:T(8,128)S(1)}, u32[]{:S(2)}, u32[]{:S(2)}) collective-permute-start(f32[16,16,384]{2,1,0:T(8,128)S(1)} %all-to-all-done), channel_id=1, source_target_pairs={{0,1},{1,0},{2,3},{3,2},{4,5},{5,4},{6,7},{7,6},{8,9},{9,8},{10,11... | collective-permute-start | bytes 1179656 | tf_op jit(solution)/shard_map/ppermute | solution.py:262
  47.5 0.7 copy-start.2
  48.2 22.4 %copy-start = (f32[8,384]{1,0:T(8,128)S(1)}, f32[8,384]{1,0:T(8,128)}, u32[]{:S(2)}) copy-start(f32[8,384]{1,0:T(8,128)} %singles.1) | copy-start | bytes 36868

commit v3 on v2

v3 whole, which is shorter than its diff:
```python
import jax
import jax.numpy as jnp
from jax import lax
from jax.experimental import pallas as pl
from jax.experimental.pallas import tpu as pltpu
from jax.sharding import PartitionSpec as P

ROW, COL, CHIPS = 16, 32, 16
SLICE = 8
D, HEADS, WIDTH = 384, 16, 24
TOKENS = 256
SLOT = 32
PAD = HEADS * SLOT
GROUP = 4
GROUPS = HEADS // GROUP
LANES = 128
TOTAL, TOP = WIDTH, WIDTH + 1
F32, BF16 = jnp.float32, jnp.bfloat16


def ring(a, b, n):
    return min((a - b) % n, (b - a) % n)


def holders(m):
    z, x_hi = divmod(m, 2)
    x_lo, y = divmod(m, 8)
    zs = sorted(range(8), key=lambda v: (-ring(v, z, 8), v))
    ys = sorted(range(8), key=lambda v: (ring(v, y, 8), v))
    out = [0] * CHIPS
    for z_from, y_to in zip(zs, ys):
        for x_from in range(2):
            out[2 * z_from + x_from] = (x_lo if x_from == x_hi else 1 - x_lo) * 8 + y_to
    return out


HOLDERS = [holders(m) for m in range(CHIPS)]
OVER_M = [[r * COL + 2 * m + k for m in range(CHIPS)] for r in range(ROW) for k in range(2)]
SIBLING = [(i, i ^ 1) for i in range(ROW * COL)]


MIXED = [[r * COL + 2 * m for m in range(CHIPS)] for r in range(ROW)] + [
    [r * COL + 2 * m + 1 for r in HOLDERS[m]] for m in range(CHIPS)
]
TO_COLUMN = [(m * COL + 2 * s, HOLDERS[m][s] * COL + 2 * m + 1) for m in range(CHIPS) for s in range(CHIPS)]


AXES = ("row", "col")


def exchange(pieces, groups):
    return lax.all_to_all(pieces, AXES, 0, 0, tiled=True, axis_index_groups=groups)


def layer_norm(rows):
    mean = jnp.mean(rows, axis=-1, keepdims=True)
    centred = rows - mean
    var = jnp.mean(centred * centred, axis=-1, keepdims=True)
    return centred * lax.rsqrt(var + 1e-05)


def split(array):
    high = array.astype(BF16)
    return high, (array - high.astype(F32)).astype(BF16)


def dot(a, b):
    return lax.dot_general(a, b, (((1,), (0,)), ((), ())), preferred_element_type=F32)


def dot_t(a, b):
    return lax.dot_general(a, b, (((1,), (1,)), ((), ())), preferred_element_type=F32)


def left(high, low):
    return jnp.concatenate((high, low, high), 1)


def right(high, low, dim=1):
    return jnp.concatenate((high, high, low), dim)


def iota(shape, dim):
    return lax.broadcasted_iota(jnp.int32, shape, dim)


def pad_heads(rows, out):
    empty = jnp.zeros((SLOT - WIDTH, D), BF16)
    for h in range(HEADS):
        out[SLOT * h : SLOT * (h + 1), :] = jnp.concatenate((rows[WIDTH * h : WIDTH * (h + 1)], empty))


def fetch(sources, targets, sems):
    copies = [pltpu.make_async_copy(a, b, sems.at[i]) for i, (a, b) in enumerate(zip(sources, targets))]
    for copy in copies:
        copy.start()
    return copies


def prepare_kernel(
    core_ref, pair, gain, w_gate, w_query, w_key, w_value, w_out, bias,
    wt_h, wt_l, wo_h, wo_l, gate, theirs, gain_in, held, gate_h, gate_l, half, sems,
):
    core = core_ref[0]
    weights = (w_gate, w_query, w_key, w_value, w_out)
    copies = fetch((gain, *weights), [gain_in] + [held.at[i] for i in range(5)], sems)
    out = pltpu.make_async_copy(bias.at[:, :, 1 - core], half, sems.at[6])
    out.start()
    copies[0].wait()
    normed = split(layer_norm(pair[:SLICE]) * gain_in[...])
    copies[1].wait()
    high, low = split(held[0].T)
    pad_heads(high, gate_h)
    pad_heads(low, gate_l)
    gate[...] = jax.nn.sigmoid(dot_t(left(*normed), right(gate_h[...], gate_l[...])))
    for i in range(3):
        copies[i + 2].wait()
        at = pl.ds(i * PAD, PAD)
        high, low = split(held[i + 1].T * gain_in[...])
        pad_heads(high, wt_h.at[at])
        pad_heads(low, wt_l.at[at])
        if i == 1:
            out.wait()
            back = pltpu.make_async_copy(half, theirs, sems.at[7])
            back.start()
    copies[5].wait()
    high, low = split(held[4])
    pad_heads(high, wo_h)
    pad_heads(low, wo_l)
    back.wait()


def in_hbm(*arrays):
    return [pltpu.with_memory_space_constraint(array, pltpu.HBM) for array in arrays]


def prepare(core, pair, gain, weights, bias):
    vmem, hbm = pl.BlockSpec(memory_space=pltpu.VMEM), pl.BlockSpec(memory_space=pl.ANY)
    part = (HEADS, CHIPS, SLICE, LANES)
    return pl.pallas_call(
        prepare_kernel,
        out_shape=[pltpu.VMEM(s, BF16) for s in [(3 * PAD, D)] * 2 + [(PAD, D)] * 2]
        + [pltpu.VMEM((SLICE, PAD), F32), pltpu.HBM(part, F32)],
        in_specs=[pl.BlockSpec(memory_space=pltpu.SMEM)] + [vmem] + [hbm] * 7,
        out_specs=[vmem] * 5 + [hbm],
        scratch_shapes=[pltpu.VMEM((1, D), F32), pltpu.VMEM((5, D, D), F32)]
        + [pltpu.VMEM((PAD, D), BF16)] * 2
        + [pltpu.VMEM(part, F32), pltpu.SemaphoreType.DMA((8,))],
        compiler_params=pltpu.CompilerParams(vmem_limit_bytes=20 << 20),
        cost_estimate=pl.CostEstimate(flops=2 * 2304 * D * PAD, bytes_accessed=8 << 20, transcendentals=SLICE * D),
        name="prepare",
    )(core.reshape(1), pair, *in_hbm(gain.reshape(1, D), *weights, bias.reshape(HEADS, CHIPS, 2, SLICE, LANES)))


def attend_kernel(core_ref, block, swapped, wt_h, wt_l, bias, other, out, held, sems):
    core = core_ref[0]
    copies = []
    for g in range(GROUPS):
        heads = pl.ds(g * GROUP, GROUP)
        pair = [
            pltpu.make_async_copy(source, held.at[at, heads], sems.at[g, i])
            for i, (source, at) in enumerate(((bias.at[heads, :, core], core), (other.at[heads], 1 - core)))
        ]
        for copy in pair:
            copy.start()
        copies.append(pair)
    first = core == 0
    own, given = block[...], swapped[...]
    q_rows = jnp.where(first, block[:, pl.ds(core, 1)], swapped[:, pl.ds(core, 1)]).reshape(TOKENS // 2, D)
    k_rows = jnp.where(first, given, own).reshape(TOKENS, D)
    q_norm = right(*split(layer_norm(q_rows)))
    k_norm = right(*split(layer_norm(k_rows)))
    half = TOKENS // 2
    queries = dot_t(left(wt_h[:PAD], wt_l[:PAD]), q_norm) * (1.0 / WIDTH**0.5)
    pairs = dot_t(left(wt_h[PAD:], wt_l[PAD:]), k_norm)
    slot = lax.shift_right_logical(iota((half, LANES), 1), 5)
    within = iota((half, LANES), 1) & (SLOT - 1)
    ones = jnp.where((iota((LANES, TOKENS), 0) & (SLOT - 1)) == TOTAL, 1.0, 0.0).astype(F32)
    for g in range(GROUPS):
        at = g * LANES
        query_h, query_l = split(queries[at : at + LANES].T)
        key = right(*split(pairs[at : at + LANES]), 0)
        value_h, value_l = split(pairs[PAD + at : PAD + at + LANES] + ones)
        zero = jnp.zeros_like(query_h)
        lhs_h = jnp.concatenate([jnp.where(slot == p, query_h, zero) for p in range(GROUP)])
        lhs_l = jnp.concatenate([jnp.where(slot == p, query_l, zero) for p in range(GROUP)])
        scores = dot(left(lhs_h, lhs_l), key)
        for copy in copies[g]:
            copy.wait()
        tops, parts_h, parts_l = [], [], []
        for p in range(GROUP):
            h = g * GROUP + p
            added = jnp.concatenate([held[k, h].reshape(half, LANES) for k in range(2)], 1)
            one = scores[p * half : (p + 1) * half] + added
            top = jnp.max(one, axis=-1, keepdims=True)
            part_h, part_l = split(jnp.exp(one - top))
            tops.append(top)
            parts_h.append(part_h)
            parts_l.append(part_l)
        sums = dot_t(jnp.concatenate(parts_h), jnp.concatenate((value_h, value_l)))
        sums = sums[:, :LANES] + (sums[:, LANES:] + dot_t(jnp.concatenate(parts_l), value_h))
        tile = jnp.zeros((half, LANES), F32)
        for p in range(GROUP):
            one = jnp.where(within == TOP, tops[p], sums[p * half : (p + 1) * half])
            tile = jnp.where(slot == p, one, tile)
        out[:, :, g * LANES : (g + 1) * LANES] = tile.reshape(CHIPS, SLICE, LANES)


def attend(core, block, swapped, weights, bias, other):
    vmem, hbm = pl.BlockSpec(memory_space=pltpu.VMEM), pl.BlockSpec(memory_space=pl.ANY)
    shape = (CHIPS, 2, SLICE, D)
    tiles = (HEADS, CHIPS, 2, SLICE, LANES)
    return pl.pallas_call(
        attend_kernel,
        out_shape=jax.ShapeDtypeStruct((CHIPS, SLICE, PAD), F32),
        in_specs=[pl.BlockSpec(memory_space=pltpu.SMEM)] + [vmem] * 4 + [hbm] * 2,
        out_specs=vmem,
        scratch_shapes=[pltpu.VMEM((2, HEADS, CHIPS, SLICE, LANES), F32), pltpu.SemaphoreType.DMA((GROUPS, 2))],
        compiler_params=pltpu.CompilerParams(vmem_limit_bytes=20 << 20),
        cost_estimate=pl.CostEstimate(flops=10**9, bytes_accessed=6 << 20, transcendentals=HEADS * 2**15),
        name="attend",
    )(core.reshape(1), block.reshape(shape), swapped.reshape(shape), *weights, *in_hbm(bias.reshape(tiles)), other)


def finish_kernel(parts, gate, wo_h, wo_l, singles, out):
    lane = iota((CHIPS * SLICE, LANES), 1)
    tops_at = lane - (lane & (SLOT - 1)) + TOP
    totals_at = tops_at[:SLICE] - TOP + TOTAL
    gated = []
    for g in range(GROUPS):
        cols = slice(g * LANES, (g + 1) * LANES)
        part = parts[:, :, cols]
        tops = jnp.take_along_axis(part.reshape(CHIPS * SLICE, LANES), tops_at, axis=1).reshape(CHIPS, SLICE, LANES)
        share = jnp.exp(tops - jnp.max(tops, axis=0, keepdims=True))
        sums = jnp.sum(part * share, axis=0)
        totals = jnp.take_along_axis(sums, totals_at, axis=1)
        gated.append(sums / totals * gate[:, cols])
    out[...] = singles[...] + dot(left(*split(jnp.concatenate(gated, 1))), right(wo_h[...], wo_l[...], 0))


def finish(*args):
    return pl.pallas_call(
        finish_kernel,
        out_shape=jax.ShapeDtypeStruct((SLICE, D), F32),
        compiler_params=pltpu.CompilerParams(vmem_limit_bytes=4 << 20),
        cost_estimate=pl.CostEstimate(flops=6 * SLICE * PAD * D, bytes_accessed=2 << 20, transcendentals=CHIPS * SLICE * PAD),
        name="finish",
    )(*args)


def body(singles, norm_gain, w_query, w_key, w_value, w_gate, w_out, pair_bias):
    core = lax.axis_index("col") % 2
    beside = lax.ppermute(singles, AXES, SIBLING)
    pair = jnp.concatenate((singles, beside))
    moved = lax.ppermute(pair, AXES, TO_COLUMN)
    *ready, theirs = prepare(core, pair, norm_gain, (w_gate, w_query, w_key, w_value, w_out), pair_bias)
    other = lax.ppermute(theirs, AXES, SIBLING)
    moved, *ready = lax.optimization_barrier((moved, *ready))
    wt_h, wt_l, wo_h, wo_l, gate = ready
    piece = jnp.where(core == 0, pair, moved)
    block = exchange(jnp.broadcast_to(piece[None], (CHIPS, 2 * SLICE, D)), MIXED)
    swapped = lax.ppermute(block, AXES, SIBLING)
    message = attend(core, block, swapped, (wt_h, wt_l), pair_bias, other)
    parts = exchange(message, OVER_M)
    return finish(parts, gate, wo_h, wo_l, singles)


def solution(mesh):
    return jax.shard_map(
        body,
        mesh=mesh,
        in_specs=(P(("row", "col"), None), P(), P(), P(), P(), P(), P(), P(None, "row", "col")),
        out_specs=P(("row", "col"), None),
        check_vma=False,
    )
```

time: 72.2 us -> 69.5 us (0.963)
  the two profiles are of different devices: /device:TPU:2 before, /device:TPU:1 now
where the time goes in v3:
time: 69.5 us; the launch traced here: 69.1 us
  starting transfers between devices  23.9 us (34%)
  blocking collectives  22.8 us (33%)
  waiting for transfers between devices  10.8 us (16%)
  Pallas kernels  8.82 us (13%)
  local copies, waits for them, and re-layouts  2.73 us (4%)
    all_to_all x1, blocking collectives, exchange(): lax.all_to_all(pieces, AXES, 0, 0, tiled=True, axis_index_groups=groups)  22.8 us
    ppermute x1, starting transfers between devices, body(): beside = lax.ppermute(singles, AXES, SIBLING)  8.78 us
    all_to_all x1, starting transfers between devices, exchange(): lax.all_to_all(pieces, AXES, 0, 0, tiled=True, axis_index_groups=groups)  6.66 us
    ppermute x1, starting transfers between devices, body(): swapped = lax.ppermute(block, AXES, SIBLING)  5.3 us
    all_to_all x1, waiting for transfers between devices, exchange(): lax.all_to_all(pieces, AXES, 0, 0, tiled=True, axis_index_groups=groups)  4.92 us
    ppermute x1, waiting for transfers between devices, body(): moved = lax.ppermute(pair, AXES, TO_COLUMN)  4.57 us
    pallas_call x1, Pallas kernels, attend(): pl.pallas_call(attend_kernel, out_shape=jax.ShapeDtypeStruct((CHIPS, SLIC...  4.56 us
    pallas_call x1, Pallas kernels, prepare(): pl.pallas_call(prepare_kernel, out_shape=[pltpu.VMEM(s, BF16) for s in [(...  3.18 us
  transfers between devices with their start and end apart: 5, of which 3 were waited for; matrix products, arithmetic and copies ran while one was open for 3% of the time, Pallas kernels for 5%

profile of v3, /device:TPU:1, one launch (start us, length us, event | category | flops | bytes accessed | tf_op | source)
XLA Modules:
  0.0 69.1 jit_solution(13478865518866047223)
XLA Ops:
  0.0 8.8 %collective-permute-start = (f32[8,384]{1,0:T(8,128)}, f32[8,384]{1,0:T(8,128)S(1)}, u32[]{:S(2)}, u32[]{:S(2)}) collective-permute-start(f32[8,384]{1,0:T(8,128)} %singles.1), channel_id=1, source_target_pairs={{0,1},{1,0},{2,3},{3,2},{4,5},{5,4},{6,7},{7,6},{8,9},{9,8},{10,11... | collective-permute-start | bytes 36872 | tf_op jit(solution)/shard_map/ppermute | solution.py:253
  8.8 0.7 %constant_dynamic-update-slice_fusion.1 = f32[16,384]{1,0:T(8,128)S(1)} fusion(f32[8,384]{1,0:T(8,128)} %singles.1), kind=kLoop, calls=%fused_computation.2 | loop fusion | bytes 24576
  9.5 1.2 %reshape.19.gain = f32[1,384]{1,0:T(1,128)} reshape(f32[384]{0:T(512)} %param.9) | data formatting | bytes 3072 | tf_op jit(solution)/shard_map/reshape | solution.py:152
  10.7 0.0 collective-permute-done
  10.7 1.3 %collective-permute-start.1 = (f32[16,384]{1,0:T(8,128)S(1)}, f32[16,384]{1,0:T(8,128)S(1)}, u32[]{:S(2)}, u32[]{:S(2)}) collective-permute-start(f32[16,384]{1,0:T(8,128)S(1)} %constant_dynamic-update-slice_fusion.pair), channel_id=1, source_target_pairs={{0,129},{2,385},{4,97},{6,353},{8,65},{10,321},{12,33},{14,289},{1... | collective-permute-start | bytes 73736 | tf_op jit(solution)/shard_map/ppermute | solution.py:255
  12.0 3.2 %prepare.1 = (bf16[1536,384]{1,0:T(8,128)(2,1)S(1)}, bf16[1536,384]{1,0:T(8,128)(2,1)S(1)}, bf16[512,384]{1,0:T(8,128)(2,1)S(1)}, bf16[512,384]{1,0:T(8,128)(2,1...) custom-call(s32[1]{0:T(128)} %bitcast.core_ref, f32[16,384]{1,0:T(8,128)S(1)} %constant_dynamic-update-slice_fusion.pair, ...), custom_call_target="tpu_custom_call" | custom-call | flops 905969664 | bytes 8388608 | tf_op jit(solution)/shard_map/prepare/pallas_call | solution.py:140
  15.2 4.6 %collective-permute-done.1 = f32[16,384]{1,0:T(8,128)S(1)} collective-permute-done((f32[16,384]{1,0:T(8,128)S(1)}, f32[16,384]{1,0:T(8,128)S(1)}, u32[]{:S(2)}, u32[]{:S(2)}) %collective-permute-start.1) | collective-permute-done | bytes 24608 | tf_op jit(solution)/shard_map/ppermute | solution.py:255
  19.8 0.8 %broadcast_in_dim.2 = f32[16,16,384]{2,1,0:T(8,128)} broadcast(f32[16,384]{1,0:T(8,128)S(1)} %broadcast_select_fusion), dimensions={1,2} | broadcast | bytes 417792 | tf_op jit(solution)/shard_map/broadcast_in_dim | solution.py:261
  20.6 6.7 %all-to-all-start = ((f32[16,16,384]{2,1,0:T(8,128)}), f32[16,16,384]{2,1,0:T(8,128)S(1)}, u32[]{:S(2)}, u32[]{:S(2)}) async-start(f32[16,16,384]{2,1,0:T(8,128)} %broadcast_in_dim.2), calls=%async_computation | async-start | bytes 786432 | tf_op jit(solution)/shard_map/all_to_all | solution.py:52
  27.2 1.9 %collective-permute-start.3 = (f32[16,16,8,128]{3,2,1,0:T(8,128)}, f32[16,16,8,128]{3,2,1,0:T(8,128)}, u32[]{:S(2)}, u32[]{:S(2)}) collective-permute-start(f32[16,16,8,128]{3,2,1,0:T(8,128)} %get-tuple-element.25), channel_id=1, source_target_pairs={{0,1},{1,0},{2,3},{3,2},{4,5},{5,4},{6,7},{7,6},{8,9},{9,8},{10,11... | collective-permute-start | bytes 3145736 | tf_op jit(solution)/shard_map/ppermute | solution.py:257
  29.1 4.9 %all-to-all-done = f32[16,16,384]{2,1,0:T(8,128)S(1)} async-done(((f32[16,16,384]{2,1,0:T(8,128)}), f32[16,16,384]{2,1,0:T(8,128)S(1)}, u32[]{:S(2)}, u32[]{:S(2)}) %all-to-all-start) | async-done | bytes 393248 | tf_op jit(solution)/shard_map/all_to_all | solution.py:52
  34.1 5.3 %collective-permute-start.2 = (f32[16,16,384]{2,1,0:T(8,128)S(1)}, f32[16,16,384]{2,1,0:T(8,128)S(1)}, u32[]{:S(2)}, u32[]{:S(2)}) collective-permute-start(f32[16,16,384]{2,1,0:T(8,128)S(1)} %all-to-all-done), channel_id=1, source_target_pairs={{0,1},{1,0},{2,3},{3,2},{4,5},{5,4},{6,7},{7,6},{8,9},{9,8},{10,11... | collective-permute-start | bytes 1179656 | tf_op jit(solution)/shard_map/ppermute | solution.py:262
  39.4 0.0 collective-permute-done.3.other
  39.4 1.3 %collective-permute-done.2 = f32[16,16,384]{2,1,0:T(8,128)S(1)} collective-permute-done((f32[16,16,384]{2,1,0:T(8,128)S(1)}, f32[16,16,384]{2,1,0:T(8,128)S(1)}, u32[]{:S(2)}, u32[]{:S(2)}) %collective-permute-start.2) | collective-permute-done | bytes 393248 | tf_op jit(solution)/shard_map/ppermute | solution.py:262
  40.7 0.0 copy-start
  40.7 4.6 %attend.1 = f32[16,8,512]{2,1,0:T(8,128)S(1)} custom-call(s32[1]{0:T(128)} %bitcast.core_ref, f32[16,2,8,384]{3,2,1,0:T(8,128)S(1)} %bitcast.4, f32[16,2,8,384]{3,2,1,0:T(8,128)S(1)} %bitcast.5, bf16[1536,384]{1,0:T(8,128)(2,1)S(1)} %get-tuple-element.23.wt_h, bf16[1536,384]{1,0:T(8,128)(2,1)S(1)} %get-tuple-element.24.wt_l, f32[16,16,2,8,128]{4,3,2,1,0:T(8,128)} %bitcast.7, ...), custom_call_target="tpu_custom_call" | custom-call | flops 1000000000 | bytes 6291456 | tf_op jit(solution)/shard_map/attend/pallas_call | solution.py:213
  45.3 22.8 %all_to_all.10.parts = f32[16,8,512]{2,1,0:T(8,128)S(1)} all-to-all(f32[16,8,512]{2,1,0:T(8,128)S(1)} %attend.1), channel_id=1, replica_groups={{0,2,4,6,8,10,12,14,16,18,20,22,24,26,28,30},{1,3,5,7,9,11,13,15,17,19,..., dimensions={0} | all-to-all | bytes 524288 | tf_op jit(solution)/shard_map/all_to_all | solution.py:52
  68.0 0.0 copy-done
  68.0 1.1 %finish.1 = f32[8,384]{1,0:T(8,128)} custom-call(f32[16,8,512]{2,1,0:T(8,128)S(1)} %all_to_all.10.parts, f32[8,512]{1,0:T(8,128)S(1)} %get-tuple-element.26.gate, bf16[512,384]{1,0:T(8,128)(2,1)S(1)} %get-tuple-element.27.wo_h, bf16[512,384]{1,0:T(8,128)(2,1)S(1)} %get-tuple-element.28.wo_l, f32[8,384]{1,0:T(8,128)S(1)} %copy-done), custom_call_target="tpu_custom_call" | custom-call | flops 9437184 | bytes 2097152 | tf_op jit(solution)/shard_map/finish/pallas_call | solution.py:242
  (2 shorter events, 0.0 us)
Async XLA Ops:
  0.0 10.7 %collective-permute-start = (f32[8,384]{1,0:T(8,128)}, f32[8,384]{1,0:T(8,128)S(1)}, u32[]{:S(2)}, u32[]{:S(2)}) collective-permute-start(f32[8,384]{1,0:T(8,128)} %singles.1), channel_id=1, source_target_pairs={{0,1},{1,0},{2,3},{3,2},{4,5},{5,4},{6,7},{7,6},{8,9},{9,8},{10,11... | collective-permute-start | bytes 36872 | tf_op jit(solution)/shard_map/ppermute | solution.py:253
  10.7 9.0 %collective-permute-start.1 = (f32[16,384]{1,0:T(8,128)S(1)}, f32[16,384]{1,0:T(8,128)S(1)}, u32[]{:S(2)}, u32[]{:S(2)}) collective-permute-start(f32[16,384]{1,0:T(8,128)S(1)} %constant_dynamic-update-slice_fusion.pair), channel_id=1, source_target_pairs={{0,129},{2,385},{4,97},{6,353},{8,65},{10,321},{12,33},{14,289},{1... | collective-permute-start | bytes 73736 | tf_op jit(solution)/shard_map/ppermute | solution.py:255
  20.6 13.5 %all-to-all-start = ((f32[16,16,384]{2,1,0:T(8,128)}), f32[16,16,384]{2,1,0:T(8,128)S(1)}, u32[]{:S(2)}, u32[]{:S(2)}) async-start(f32[16,16,384]{2,1,0:T(8,128)} %broadcast_in_dim.2), calls=%async_computation | async-start | bytes 786432 | tf_op jit(solution)/shard_map/all_to_all | solution.py:52
  27.2 12.1 %collective-permute-start.3 = (f32[16,16,8,128]{3,2,1,0:T(8,128)}, f32[16,16,8,128]{3,2,1,0:T(8,128)}, u32[]{:S(2)}, u32[]{:S(2)}) collective-permute-start(f32[16,16,8,128]{3,2,1,0:T(8,128)} %get-tuple-element.25), channel_id=1, source_target_pairs={{0,1},{1,0},{2,3},{3,2},{4,5},{5,4},{6,7},{7,6},{8,9},{9,8},{10,11... | collective-permute-start | bytes 3145736 | tf_op jit(solution)/shard_map/ppermute | solution.py:257
  34.1 6.6 %collective-permute-start.2 = (f32[16,16,384]{2,1,0:T(8,128)S(1)}, f32[16,16,384]{2,1,0:T(8,128)S(1)}, u32[]{:S(2)}, u32[]{:S(2)}) collective-permute-start(f32[16,16,384]{2,1,0:T(8,128)S(1)} %all-to-all-done), channel_id=1, source_target_pairs={{0,1},{1,0},{2,3},{3,2},{4,5},{5,4},{6,7},{7,6},{8,9},{9,8},{10,11... | collective-permute-start | bytes 1179656 | tf_op jit(solution)/shard_map/ppermute | solution.py:262
  40.7 27.3 %copy-start = (f32[8,384]{1,0:T(8,128)S(1)}, f32[8,384]{1,0:T(8,128)}, u32[]{:S(2)}) copy-start(f32[8,384]{1,0:T(8,128)} %singles.1) | copy-start | bytes 36868

commit v4 on v3

--- a/solution.py
+++ b/solution.py
@@ -98,36 +98,36 @@
 
 
 def prepare_kernel(
-    core_ref, pair, gain, w_gate, w_query, w_key, w_value, w_out, bias,
-    wt_h, wt_l, wo_h, wo_l, gate, theirs, gain_in, held, gate_h, gate_l, half, sems,
+    core_ref, pair, gain, w_out, w_gate, w_query, w_key, w_value, bias,
+    wt_h, wt_l, wo_h, wo_l, gate, theirs, gain_in, held, gate_h, gate_l, out_h, out_l, half, sems,
 ):
     core = core_ref[0]
-    weights = (w_gate, w_query, w_key, w_value, w_out)
-    copies = fetch((gain, *weights), [gain_in] + [held.at[i] for i in range(5)], sems)
+    weights = (w_out, w_gate, w_query, w_key, w_value)
+    copies = fetch((gain, *weights), [gain_in.at[0]] + [held.at[i] for i in range(5)], sems)
     out = pltpu.make_async_copy(bias.at[:, :, 1 - core], half, sems.at[6])
     out.start()
     copies[0].wait()
     normed = split(layer_norm(pair[:SLICE]) * gain_in[...])
     copies[1].wait()
-    high, low = split(held[0].T)
+    high, low = split(held[0])
+    pad_heads(high, out_h)
+    pad_heads(low, out_l)
+    backs = fetch((out_h, out_l), (wo_h, wo_l), sems.at[pl.ds(8, 2)])
+    copies[2].wait()
+    high, low = split(held[1].T)
     pad_heads(high, gate_h)
     pad_heads(low, gate_l)
     gate[...] = jax.nn.sigmoid(dot_t(left(*normed), right(gate_h[...], gate_l[...])))
     for i in range(3):
-        copies[i + 2].wait()
-        at = pl.ds(i * PAD, PAD)
-        high, low = split(held[i + 1].T * gain_in[...])
-        pad_heads(high, wt_h.at[at])
-        pad_heads(low, wt_l.at[at])
+        copies[i + 3].wait()
+        at = pl.ds(i * D, D)
+        wt_h[at], wt_l[at] = split(held[i + 2].T * gain_in[...])
         if i == 1:
             out.wait()
             back = pltpu.make_async_copy(half, theirs, sems.at[7])
             back.start()
-    copies[5].wait()
-    high, low = split(held[4])
-    pad_heads(high, wo_h)
-    pad_heads(low, wo_l)
-    back.wait()
+    for copy in (back, *backs):
+        copy.wait()
 
 
 def in_hbm(*arrays):
@@ -139,31 +139,42 @@
     part = (HEADS, CHIPS, SLICE, LANES)
     return pl.pallas_call(
         prepare_kernel,
-        out_shape=[pltpu.VMEM(s, BF16) for s in [(3 * PAD, D)] * 2 + [(PAD, D)] * 2]
+        out_shape=[pltpu.VMEM((3 * D, D), BF16)] * 2
+        + [pltpu.HBM((PAD, D), BF16)] * 2
         + [pltpu.VMEM((SLICE, PAD), F32), pltpu.HBM(part, F32)],
         in_specs=[pl.BlockSpec(memory_space=pltpu.SMEM)] + [vmem] + [hbm] * 7,
-        out_specs=[vmem] * 5 + [hbm],
+        out_specs=[vmem] * 2 + [hbm] * 2 + [vmem, hbm],
         scratch_shapes=[pltpu.VMEM((1, D), F32), pltpu.VMEM((5, D, D), F32)]
-        + [pltpu.VMEM((PAD, D), BF16)] * 2
-        + [pltpu.VMEM(part, F32), pltpu.SemaphoreType.DMA((8,))],
+        + [pltpu.VMEM((PAD, D), BF16)] * 4
+        + [pltpu.VMEM(part, F32), pltpu.SemaphoreType.DMA((10,))],
         compiler_params=pltpu.CompilerParams(vmem_limit_bytes=20 << 20),
         cost_estimate=pl.CostEstimate(flops=2 * 2304 * D * PAD, bytes_accessed=8 << 20, transcendentals=SLICE * D),
         name="prepare",
-    )(core.reshape(1), pair, *in_hbm(gain.reshape(1, D), *weights, bias.reshape(HEADS, CHIPS, 2, SLICE, LANES)))
-
-
-def attend_kernel(core_ref, block, swapped, wt_h, wt_l, bias, other, out, held, sems):
+    )(core.reshape(1), pair, *in_hbm(gain, *weights, bias.reshape(HEADS, CHIPS, 2, SLICE, LANES)))
+
+
+def stage_kernel(core_ref, bias, other, held, sems):
     core = core_ref[0]
-    copies = []
-    for g in range(GROUPS):
-        heads = pl.ds(g * GROUP, GROUP)
-        pair = [
-            pltpu.make_async_copy(source, held.at[at, heads], sems.at[g, i])
-            for i, (source, at) in enumerate(((bias.at[heads, :, core], core), (other.at[heads], 1 - core)))
-        ]
-        for copy in pair:
-            copy.start()
-        copies.append(pair)
+    for copy in fetch((bias.at[:, :, core], other), (held.at[core], held.at[1 - core]), sems):
+        copy.wait()
+
+
+def stage(core, bias, other):
+    hbm = pl.BlockSpec(memory_space=pl.ANY)
+    return pl.pallas_call(
+        stage_kernel,
+        out_shape=pltpu.VMEM((2, HEADS, CHIPS, SLICE, LANES), F32),
+        in_specs=[pl.BlockSpec(memory_space=pltpu.SMEM)] + [hbm] * 2,
+        out_specs=pl.BlockSpec(memory_space=pltpu.VMEM),
+        scratch_shapes=[pltpu.SemaphoreType.DMA((2,))],
+        compiler_params=pltpu.CompilerParams(vmem_limit_bytes=20 << 20),
+        cost_estimate=pl.CostEstimate(flops=0, bytes_accessed=4 << 20, transcendentals=0),
+        name="stage",
+    )(core.reshape(1), *in_hbm(bias.reshape(HEADS, CHIPS, 2, SLICE, LANES)), other)
+
+
+def attend_kernel(core_ref, block, swapped, wt_h, wt_l, held, out):
+    core = core_ref[0]
     first = core == 0
     own, given = block[...], swapped[...]
     q_rows = jnp.where(first, block[:, pl.ds(core, 1)], swapped[:, pl.ds(core, 1)]).reshape(TOKENS // 2, D)
@@ -171,22 +182,29 @@
     q_norm = right(*split(layer_norm(q_rows)))
     k_norm = right(*split(layer_norm(k_rows)))
     half = TOKENS // 2
-    queries = dot_t(left(wt_h[:PAD], wt_l[:PAD]), q_norm) * (1.0 / WIDTH**0.5)
-    pairs = dot_t(left(wt_h[PAD:], wt_l[PAD:]), k_norm)
+    queries = dot_t(left(wt_h[:D], wt_l[:D]), q_norm) * (1.0 / WIDTH**0.5)
+    pairs = dot_t(left(wt_h[D:], wt_l[D:]), k_norm)
     slot = lax.shift_right_logical(iota((half, LANES), 1), 5)
     within = iota((half, LANES), 1) & (SLOT - 1)
-    ones = jnp.where((iota((LANES, TOKENS), 0) & (SLOT - 1)) == TOTAL, 1.0, 0.0).astype(F32)
+    blank = jnp.zeros((SLOT - WIDTH, half), F32)
+    blank_key = jnp.zeros((SLOT - WIDTH, TOKENS), F32)
+    ones = jnp.where(iota((SLOT - WIDTH, TOKENS), 0) == TOTAL - WIDTH, 1.0, 0.0).astype(F32)
+
+    def slots(rows, first, filler):
+        parts = []
+        for p in range(GROUP):
+            parts += [rows[first + p * WIDTH : first + (p + 1) * WIDTH], filler]
+        return jnp.concatenate(parts)
+
     for g in range(GROUPS):
-        at = g * LANES
-        query_h, query_l = split(queries[at : at + LANES].T)
-        key = right(*split(pairs[at : at + LANES]), 0)
-        value_h, value_l = split(pairs[PAD + at : PAD + at + LANES] + ones)
+        at = g * GROUP * WIDTH
+        query_h, query_l = split(slots(queries, at, blank).T)
+        key = right(*split(slots(pairs, at, blank_key)), 0)
+        value_h, value_l = split(slots(pairs, D + at, ones))
         zero = jnp.zeros_like(query_h)
         lhs_h = jnp.concatenate([jnp.where(slot == p, query_h, zero) for p in range(GROUP)])
         lhs_l = jnp.concatenate([jnp.where(slot == p, query_l, zero) for p in range(GROUP)])
         scores = dot(left(lhs_h, lhs_l), key)
-        for copy in copies[g]:
-            copy.wait()
         tops, parts_h, parts_l = [], [], []
         for p in range(GROUP):
             h = g * GROUP + p
@@ -206,20 +224,18 @@
         out[:, :, g * LANES : (g + 1) * LANES] = tile.reshape(CHIPS, SLICE, LANES)
 
 
-def attend(core, block, swapped, weights, bias, other):
-    vmem, hbm = pl.BlockSpec(memory_space=pltpu.VMEM), pl.BlockSpec(memory_space=pl.ANY)
+def attend(core, block, swapped, weights, staged):
+    vmem = pl.BlockSpec(memory_space=pltpu.VMEM)
     shape = (CHIPS, 2, SLICE, D)
-    tiles = (HEADS, CHIPS, 2, SLICE, LANES)
     return pl.pallas_call(
         attend_kernel,
         out_shape=jax.ShapeDtypeStruct((CHIPS, SLICE, PAD), F32),
-        in_specs=[pl.BlockSpec(memory_space=pltpu.SMEM)] + [vmem] * 4 + [hbm] * 2,
+        in_specs=[pl.BlockSpec(memory_space=pltpu.SMEM)] + [vmem] * 5,
         out_specs=vmem,
-        scratch_shapes=[pltpu.VMEM((2, HEADS, CHIPS, SLICE, LANES), F32), pltpu.SemaphoreType.DMA((GROUPS, 2))],
         compiler_params=pltpu.CompilerParams(vmem_limit_bytes=20 << 20),
         cost_estimate=pl.CostEstimate(flops=10**9, bytes_accessed=6 << 20, transcendentals=HEADS * 2**15),
         name="attend",
-    )(core.reshape(1), block.reshape(shape), swapped.reshape(shape), *weights, *in_hbm(bias.reshape(tiles)), other)
+    )(core.reshape(1), block.reshape(shape), swapped.reshape(shape), *weights, staged)
 
 
 def finish_kernel(parts, gate, wo_h, wo_l, singles, out):
@@ -235,7 +251,9 @@
         sums = jnp.sum(part * share, axis=0)
         totals = jnp.take_along_axis(sums, totals_at, axis=1)
         gated.append(sums / totals * gate[:, cols])
-    out[...] = singles[...] + dot(left(*split(jnp.concatenate(gated, 1))), right(wo_h[...], wo_l[...], 0))
+    high, low = split(jnp.concatenate(gated, 1))
+    both = dot(jnp.concatenate((high, low)), wo_h[...])
+    out[...] = singles[...] + (both[:SLICE] + (both[SLICE:] + dot(high, wo_l[...])))
 
 
 def finish(*args):
@@ -253,14 +271,13 @@
     beside = lax.ppermute(singles, AXES, SIBLING)
     pair = jnp.concatenate((singles, beside))
     moved = lax.ppermute(pair, AXES, TO_COLUMN)
-    *ready, theirs = prepare(core, pair, norm_gain, (w_gate, w_query, w_key, w_value, w_out), pair_bias)
+    wt_h, wt_l, wo_h, wo_l, gate, theirs = prepare(core, pair, norm_gain, (w_out, w_gate, w_query, w_key, w_value), pair_bias)
     other = lax.ppermute(theirs, AXES, SIBLING)
-    moved, *ready = lax.optimization_barrier((moved, *ready))
-    wt_h, wt_l, wo_h, wo_l, gate = ready
+    moved, wt_h, wt_l, gate = lax.optimization_barrier((moved, wt_h, wt_l, gate))
     piece = jnp.where(core == 0, pair, moved)
     block = exchange(jnp.broadcast_to(piece[None], (CHIPS, 2 * SLICE, D)), MIXED)
     swapped = lax.ppermute(block, AXES, SIBLING)
-    message = attend(core, block, swapped, (wt_h, wt_l), pair_bias, other)
+    message = attend(core, block, swapped, (wt_h, wt_l), stage(core, pair_bias, other))
     parts = exchange(message, OVER_M)
     return finish(parts, gate, wo_h, wo_l, singles)
 

time: 69.5 us -> 67.5 us (0.971)
  local copies, waits for them, and re-layouts: 2.73 us -> 1.53 us
  waiting for transfers between devices: 10.8 us -> 9.66 us
    pallas_call x1 -> x2, Pallas kernels: 3.18 us -> 4.63 us  [the longest x1 3.38 us: prepare(): pl.pallas_call(prepare_kernel, out_shape=[pltpu.VMEM((3 * D, D), BF16)] *...]
    ppermute x1, waiting for transfers between devices: 1.32 us -> 0.06 us  [body(): swapped = lax.ppermute(block, AXES, SIBLING)]
    reshape x1 -> x0, local copies, waits for them, and re-layouts: 1.24 us -> none  [prepare(): gain.reshape(1, D)]
    pallas_call x1, Pallas kernels: 4.56 us -> 3.52 us  [attend(): pl.pallas_call(attend_kernel, out_shape=jax.ShapeDtypeStruct((CHIPS, SLIC...]
  transfers between devices with their start and end apart: 5 -> 5, of which waited for: 3 -> 4; matrix products, arithmetic and copies ran while one was open for 3% -> 1% of each run, Pallas kernels for 5% -> 7%
where the time goes in v4:
time: 67.5 us; the launch traced here: 67.1 us
  starting transfers between devices  24.1 us (36%)
  blocking collectives  22.5 us (33%)
  waiting for transfers between devices  9.66 us (14%)
  Pallas kernels  9.18 us (14%)
  local copies, waits for them, and re-layouts  1.53 us (2%)
    all_to_all x1, blocking collectives, exchange(): lax.all_to_all(pieces, AXES, 0, 0, tiled=True, axis_index_groups=groups)  22.5 us
    ppermute x1, starting transfers between devices, body(): beside = lax.ppermute(singles, AXES, SIBLING)  8.78 us
    all_to_all x1, starting transfers between devices, exchange(): lax.all_to_all(pieces, AXES, 0, 0, tiled=True, axis_index_groups=groups)  6.66 us
    ppermute x1, starting transfers between devices, body(): swapped = lax.ppermute(block, AXES, SIBLING)  5.5 us
    all_to_all x1, waiting for transfers between devices, exchange(): lax.all_to_all(pieces, AXES, 0, 0, tiled=True, axis_index_groups=groups)  4.92 us
    ppermute x1, waiting for transfers between devices, body(): moved = lax.ppermute(pair, AXES, TO_COLUMN)  4.37 us
    pallas_call x1, Pallas kernels, attend(): pl.pallas_call(attend_kernel, out_shape=jax.ShapeDtypeStruct((CHIPS, SLIC...  3.52 us
    pallas_call x1, Pallas kernels, prepare(): pl.pallas_call(prepare_kernel, out_shape=[pltpu.VMEM((3 * D, D), BF16)] *...  3.38 us
  transfers between devices with their start and end apart: 5, of which 4 were waited for; matrix products, arithmetic and copies ran while one was open for 1% of the time, Pallas kernels for 7%

profile of v4, /device:TPU:1, one launch (start us, length us, event | category | flops | bytes accessed | tf_op | source)
XLA Modules:
  0.0 67.1 jit_solution(596084879985125932)
XLA Ops:
  0.0 8.8 %collective-permute-start = (f32[8,384]{1,0:T(8,128)}, f32[8,384]{1,0:T(8,128)S(1)}, u32[]{:S(2)}, u32[]{:S(2)}) collective-permute-start(f32[8,384]{1,0:T(8,128)} %singles.1), channel_id=1, source_target_pairs={{0,1},{1,0},{2,3},{3,2},{4,5},{5,4},{6,7},{7,6},{8,9},{9,8},{10,11... | collective-permute-start | bytes 36872 | tf_op jit(solution)/shard_map/ppermute | solution.py:271
  8.8 0.7 %constant_dynamic-update-slice_fusion.1 = f32[16,384]{1,0:T(8,128)S(1)} fusion(f32[8,384]{1,0:T(8,128)} %singles.1), kind=kLoop, calls=%fused_computation.2 | loop fusion | bytes 24576
  9.5 0.3 collective-permute-done
  9.8 1.3 %collective-permute-start.1 = (f32[16,384]{1,0:T(8,128)S(1)}, f32[16,384]{1,0:T(8,128)S(1)}, u32[]{:S(2)}, u32[]{:S(2)}) collective-permute-start(f32[16,384]{1,0:T(8,128)S(1)} %constant_dynamic-update-slice_fusion.pair), channel_id=1, source_target_pairs={{0,129},{2,385},{4,97},{6,353},{8,65},{10,321},{12,33},{14,289},{1... | collective-permute-start | bytes 73736 | tf_op jit(solution)/shard_map/ppermute | solution.py:273
  11.1 3.4 %prepare.1 = (bf16[1152,384]{1,0:T(8,128)(2,1)S(1)}, bf16[1152,384]{1,0:T(8,128)(2,1)S(1)}, bf16[512,384]{1,0:T(8,128)(2,1)}, bf16[512,384]{1,0:T(8,128)(2,1)}, ...) custom-call(s32[1]{0:T(128)} %bitcast.core_ref, f32[16,384]{1,0:T(8,128)S(1)} %constant_dynamic-update-slice_fusion.pair, ...), custom_call_target="tpu_custom_call" | custom-call | flops 905969664 | bytes 8388608 | tf_op jit(solution)/shard_map/prepare/pallas_call | solution.py:140
  14.5 4.4 %collective-permute-done.1 = f32[16,384]{1,0:T(8,128)S(1)} collective-permute-done((f32[16,384]{1,0:T(8,128)S(1)}, f32[16,384]{1,0:T(8,128)S(1)}, u32[]{:S(2)}, u32[]{:S(2)}) %collective-permute-start.1) | collective-permute-done | bytes 24608 | tf_op jit(solution)/shard_map/ppermute | solution.py:273
  18.9 0.8 %broadcast_in_dim.2 = f32[16,16,384]{2,1,0:T(8,128)} broadcast(f32[16,384]{1,0:T(8,128)S(1)} %broadcast_select_fusion), dimensions={1,2} | broadcast | bytes 417792 | tf_op jit(solution)/shard_map/broadcast_in_dim | solution.py:278
  19.7 6.7 %all-to-all-start = ((f32[16,16,384]{2,1,0:T(8,128)}), f32[16,16,384]{2,1,0:T(8,128)S(1)}, u32[]{:S(2)}, u32[]{:S(2)}) async-start(f32[16,16,384]{2,1,0:T(8,128)} %broadcast_in_dim.2), calls=%async_computation | async-start | bytes 786432 | tf_op jit(solution)/shard_map/all_to_all | solution.py:52
  26.3 1.9 %collective-permute-start.3 = (f32[16,16,8,128]{3,2,1,0:T(8,128)}, f32[16,16,8,128]{3,2,1,0:T(8,128)S(1)}, u32[]{:S(2)}, u32[]{:S(2)}) collective-permute-start(f32[16,16,8,128]{3,2,1,0:T(8,128)} %get-tuple-element.21), channel_id=1, source_target_pairs={{0,1},{1,0},{2,3},{3,2},{4,5},{5,4},{6,7},{7,6},{8,9},{9,8},{10,11... | collective-permute-start | bytes 3145736 | tf_op jit(solution)/shard_map/ppermute | solution.py:275
  28.2 4.9 %all-to-all-done = f32[16,16,384]{2,1,0:T(8,128)S(1)} async-done(((f32[16,16,384]{2,1,0:T(8,128)}), f32[16,16,384]{2,1,0:T(8,128)S(1)}, u32[]{:S(2)}, u32[]{:S(2)}) %all-to-all-start) | async-done | bytes 393248 | tf_op jit(solution)/shard_map/all_to_all | solution.py:52
  33.2 5.5 %collective-permute-start.2 = (f32[16,16,384]{2,1,0:T(8,128)S(1)}, f32[16,16,384]{2,1,0:T(8,128)S(1)}, u32[]{:S(2)}, u32[]{:S(2)}) collective-permute-start(f32[16,16,384]{2,1,0:T(8,128)S(1)} %all-to-all-done), channel_id=1, source_target_pairs={{0,1},{1,0},{2,3},{3,2},{4,5},{5,4},{6,7},{7,6},{8,9},{9,8},{10,11... | collective-permute-start | bytes 1179656 | tf_op jit(solution)/shard_map/ppermute | solution.py:279
  38.7 0.0 collective-permute-done.3.other
  38.7 1.2 %stage.1.held = f32[2,16,16,8,128]{4,3,2,1,0:T(8,128)S(1)} custom-call(s32[1]{0:T(128)} %bitcast.core_ref, f32[16,16,2,8,128]{4,3,2,1,0:T(8,128)} %bitcast.7, f32[16,16,8,128]{3,2,1,0:T(8,128)S(1)} %collective-permute-done.3.other), custom_call_target="tpu_custom_call" | custom-call | bytes 4194304 | tf_op jit(solution)/shard_map/stage/pallas_call | solution.py:164
  39.9 0.1 collective-permute-done.2
  40.0 0.0 copy-start
  40.0 0.0 copy-start.1
  40.0 0.0 copy-start.2
  40.0 3.5 %attend.1 = f32[16,8,512]{2,1,0:T(8,128)S(1)} custom-call(s32[1]{0:T(128)} %bitcast.core_ref, f32[16,2,8,384]{3,2,1,0:T(8,128)S(1)} %bitcast.4, f32[16,2,8,384]{3,2,1,0:T(8,128)S(1)} %bitcast.5, bf16[1152,384]{1,0:T(8,128)(2,1)S(1)} %get-tuple-element.19.wt_h, bf16[1152,384]{1,0:T(8,128)(2,1)S(1)} %get-tuple-element.20.wt_l, ...), custom_call_target="tpu_custom_call" | custom-call | flops 1000000000 | bytes 6291456 | tf_op jit(solution)/shard_map/attend/pallas_call | solution.py:230
  43.5 22.5 %all_to_all.10.parts = f32[16,8,512]{2,1,0:T(8,128)S(1)} all-to-all(f32[16,8,512]{2,1,0:T(8,128)S(1)} %attend.1), channel_id=1, replica_groups={{0,2,4,6,8,10,12,14,16,18,20,22,24,26,28,30},{1,3,5,7,9,11,13,15,17,19,..., dimensions={0} | all-to-all | bytes 524288 | tf_op jit(solution)/shard_map/all_to_all | solution.py:52
  66.1 0.0 copy-done
  66.1 0.0 copy-done.1
  66.1 0.0 copy-done.2
  66.1 1.0 %finish.1 = f32[8,384]{1,0:T(8,128)} custom-call(f32[16,8,512]{2,1,0:T(8,128)S(1)} %all_to_all.10.parts, f32[8,512]{1,0:T(8,128)S(1)} %get-tuple-element.22.gate, bf16[512,384]{1,0:T(8,128)(2,1)S(1)} %copy-done, bf16[512,384]{1,0:T(8,128)(2,1)S(1)} %copy-done.1, f32[8,384]{1,0:T(8,128)S(1)} %copy-done.2), custom_call_target="tpu_custom_call" | custom-call | flops 9437184 | bytes 2097152 | tf_op jit(solution)/shard_map/finish/pallas_call | solution.py:260
  (2 shorter events, 0.0 us)
Async XLA Ops:
  0.0 9.8 %collective-permute-start = (f32[8,384]{1,0:T(8,128)}, f32[8,384]{1,0:T(8,128)S(1)}, u32[]{:S(2)}, u32[]{:S(2)}) collective-permute-start(f32[8,384]{1,0:T(8,128)} %singles.1), channel_id=1, source_target_pairs={{0,1},{1,0},{2,3},{3,2},{4,5},{5,4},{6,7},{7,6},{8,9},{9,8},{10,11... | collective-permute-start | bytes 36872 | tf_op jit(solution)/shard_map/ppermute | solution.py:271
  9.8 9.0 %collective-permute-start.1 = (f32[16,384]{1,0:T(8,128)S(1)}, f32[16,384]{1,0:T(8,128)S(1)}, u32[]{:S(2)}, u32[]{:S(2)}) collective-permute-start(f32[16,384]{1,0:T(8,128)S(1)} %constant_dynamic-update-slice_fusion.pair), channel_id=1, source_target_pairs={{0,129},{2,385},{4,97},{6,353},{8,65},{10,321},{12,33},{14,289},{1... | collective-permute-start | bytes 73736 | tf_op jit(solution)/shard_map/ppermute | solution.py:273
  19.7 13.5 %all-to-all-start = ((f32[16,16,384]{2,1,0:T(8,128)}), f32[16,16,384]{2,1,0:T(8,128)S(1)}, u32[]{:S(2)}, u32[]{:S(2)}) async-start(f32[16,16,384]{2,1,0:T(8,128)} %broadcast_in_dim.2), calls=%async_computation | async-start | bytes 786432 | tf_op jit(solution)/shard_map/all_to_all | solution.py:52
  26.3 12.3 %collective-permute-start.3 = (f32[16,16,8,128]{3,2,1,0:T(8,128)}, f32[16,16,8,128]{3,2,1,0:T(8,128)S(1)}, u32[]{:S(2)}, u32[]{:S(2)}) collective-permute-start(f32[16,16,8,128]{3,2,1,0:T(8,128)} %get-tuple-element.21), channel_id=1, source_target_pairs={{0,1},{1,0},{2,3},{3,2},{4,5},{5,4},{6,7},{7,6},{8,9},{9,8},{10,11... | collective-permute-start | bytes 3145736 | tf_op jit(solution)/shard_map/ppermute | solution.py:275
  33.2 6.8 %collective-permute-start.2 = (f32[16,16,384]{2,1,0:T(8,128)S(1)}, f32[16,16,384]{2,1,0:T(8,128)S(1)}, u32[]{:S(2)}, u32[]{:S(2)}) collective-permute-start(f32[16,16,384]{2,1,0:T(8,128)S(1)} %all-to-all-done), channel_id=1, source_target_pairs={{0,1},{1,0},{2,3},{3,2},{4,5},{5,4},{6,7},{7,6},{8,9},{9,8},{10,11... | collective-permute-start | bytes 1179656 | tf_op jit(solution)/shard_map/ppermute | solution.py:279
  40.0 26.1 %copy-start = (bf16[512,384]{1,0:T(8,128)(2,1)S(1)}, bf16[512,384]{1,0:T(8,128)(2,1)}, u32[]{:S(2)}) copy-start(bf16[512,384]{1,0:T(8,128)(2,1)} %get-tuple-element.23.wo_h) | copy-start | bytes 1179652
  40.0 26.1 %copy-start.1 = (bf16[512,384]{1,0:T(8,128)(2,1)S(1)}, bf16[512,384]{1,0:T(8,128)(2,1)}, u32[]{:S(2)}) copy-start(bf16[512,384]{1,0:T(8,128)(2,1)} %get-tuple-element.24.wo_l) | copy-start | bytes 1179652
  40.0 26.1 %copy-start.2 = (f32[8,384]{1,0:T(8,128)S(1)}, f32[8,384]{1,0:T(8,128)}, u32[]{:S(2)}) copy-start(f32[8,384]{1,0:T(8,128)} %singles.1) | copy-start | bytes 36868

commit v5 on v4

--- a/solution.py
+++ b/solution.py
@@ -42,7 +42,14 @@
 MIXED = [[r * COL + 2 * m for m in range(CHIPS)] for r in range(ROW)] + [
     [r * COL + 2 * m + 1 for r in HOLDERS[m]] for m in range(CHIPS)
 ]
-TO_COLUMN = [(m * COL + 2 * s, HOLDERS[m][s] * COL + 2 * m + 1) for m in range(CHIPS) for s in range(CHIPS)]
+
+
+def to_column(core):
+    return [(m * COL + 2 * s + core, HOLDERS[m][s] * COL + 2 * m + 1) for m in range(CHIPS) for s in range(CHIPS)]
+
+
+TO_COLUMN_1 = to_column(1)
+TO_COLUMN_0 = to_column(0) + [(i, i - 1) for i in range(1, ROW * COL, 2)]
 
 
 AXES = ("row", "col")
@@ -98,16 +105,14 @@
 
 
 def prepare_kernel(
-    core_ref, pair, gain, w_out, w_gate, w_query, w_key, w_value, bias,
-    wt_h, wt_l, wo_h, wo_l, gate, theirs, gain_in, held, gate_h, gate_l, out_h, out_l, half, sems,
+    singles, gain, w_out, w_gate, w_query, w_key, w_value,
+    wt_h, wt_l, wo_h, wo_l, gate, singles_in, gain_in, held, gate_h, gate_l, out_h, out_l, sems,
 ):
-    core = core_ref[0]
     weights = (w_out, w_gate, w_query, w_key, w_value)
-    copies = fetch((gain, *weights), [gain_in.at[0]] + [held.at[i] for i in range(5)], sems)
-    out = pltpu.make_async_copy(bias.at[:, :, 1 - core], half, sems.at[6])
-    out.start()
+    copies = fetch((gain, *weights, singles), [gain_in.at[0]] + [held.at[i] for i in range(5)] + [singles_in], sems)
     copies[0].wait()
-    normed = split(layer_norm(pair[:SLICE]) * gain_in[...])
+    copies[6].wait()
+    normed = split(layer_norm(singles_in[...]) * gain_in[...])
     copies[1].wait()
     high, low = split(held[0])
     pad_heads(high, out_h)
@@ -122,11 +127,7 @@
         copies[i + 3].wait()
         at = pl.ds(i * D, D)
         wt_h[at], wt_l[at] = split(held[i + 2].T * gain_in[...])
-        if i == 1:
-            out.wait()
-            back = pltpu.make_async_copy(half, theirs, sems.at[7])
-            back.start()
-    for copy in (back, *backs):
+    for copy in backs:
         copy.wait()
 
 
@@ -134,23 +135,42 @@
     return [pltpu.with_memory_space_constraint(array, pltpu.HBM) for array in arrays]
 
 
-def prepare(core, pair, gain, weights, bias):
+def prepare(singles, gain, *weights):
     vmem, hbm = pl.BlockSpec(memory_space=pltpu.VMEM), pl.BlockSpec(memory_space=pl.ANY)
-    part = (HEADS, CHIPS, SLICE, LANES)
     return pl.pallas_call(
         prepare_kernel,
-        out_shape=[pltpu.VMEM((3 * D, D), BF16)] * 2
-        + [pltpu.HBM((PAD, D), BF16)] * 2
-        + [pltpu.VMEM((SLICE, PAD), F32), pltpu.HBM(part, F32)],
-        in_specs=[pl.BlockSpec(memory_space=pltpu.SMEM)] + [vmem] + [hbm] * 7,
-        out_specs=[vmem] * 2 + [hbm] * 2 + [vmem, hbm],
-        scratch_shapes=[pltpu.VMEM((1, D), F32), pltpu.VMEM((5, D, D), F32)]
+        out_shape=[pltpu.VMEM((3 * D, D), BF16)] * 2 + [pltpu.HBM((PAD, D), BF16)] * 2 + [pltpu.VMEM((SLICE, PAD), F32)],
+        in_specs=[hbm] * 7,
+        out_specs=[vmem] * 2 + [hbm] * 2 + [vmem],
+        scratch_shapes=[pltpu.VMEM((SLICE, D), F32), pltpu.VMEM((1, D), F32), pltpu.VMEM((5, D, D), F32)]
         + [pltpu.VMEM((PAD, D), BF16)] * 4
-        + [pltpu.VMEM(part, F32), pltpu.SemaphoreType.DMA((10,))],
+        + [pltpu.SemaphoreType.DMA((10,))],
         compiler_params=pltpu.CompilerParams(vmem_limit_bytes=20 << 20),
         cost_estimate=pl.CostEstimate(flops=2 * 2304 * D * PAD, bytes_accessed=8 << 20, transcendentals=SLICE * D),
         name="prepare",
-    )(core.reshape(1), pair, *in_hbm(gain, *weights, bias.reshape(HEADS, CHIPS, 2, SLICE, LANES)))
+    )(*in_hbm(singles, gain, *weights))
+
+
+def cut_kernel(core_ref, bias, theirs, half, sems):
+    for copy in fetch((bias.at[:, :, 1 - core_ref[0]],), (half,), sems):
+        copy.wait()
+    for copy in fetch((half,), (theirs,), sems.at[pl.ds(1, 1)]):
+        copy.wait()
+
+
+def cut(core, bias):
+    part = (HEADS, CHIPS, SLICE, LANES)
+    hbm = pl.BlockSpec(memory_space=pl.ANY)
+    return pl.pallas_call(
+        cut_kernel,
+        out_shape=pltpu.HBM(part, F32),
+        in_specs=[pl.BlockSpec(memory_space=pltpu.SMEM), hbm],
+        out_specs=hbm,
+        scratch_shapes=[pltpu.VMEM(part, F32), pltpu.SemaphoreType.DMA((2,))],
+        compiler_params=pltpu.CompilerParams(vmem_limit_bytes=20 << 20),
+        cost_estimate=pl.CostEstimate(flops=0, bytes_accessed=4 << 20, transcendentals=0),
+        name="cut",
+    )(core.reshape(1), *in_hbm(bias.reshape(HEADS, CHIPS, 2, SLICE, LANES)))
 
 
 def stage_kernel(core_ref, bias, other, held, sems):
@@ -268,14 +288,16 @@
 
 def body(singles, norm_gain, w_query, w_key, w_value, w_gate, w_out, pair_bias):
     core = lax.axis_index("col") % 2
-    beside = lax.ppermute(singles, AXES, SIBLING)
-    pair = jnp.concatenate((singles, beside))
-    moved = lax.ppermute(pair, AXES, TO_COLUMN)
-    wt_h, wt_l, wo_h, wo_l, gate, theirs = prepare(core, pair, norm_gain, (w_out, w_gate, w_query, w_key, w_value), pair_bias)
+    moved = lax.ppermute(singles, AXES, TO_COLUMN_1)
+    first = lax.ppermute(singles, AXES, TO_COLUMN_0)
+    theirs = cut(core, pair_bias)
+    moved, first, theirs = lax.optimization_barrier((moved, first, theirs))
     other = lax.ppermute(theirs, AXES, SIBLING)
-    moved, wt_h, wt_l, gate = lax.optimization_barrier((moved, wt_h, wt_l, gate))
-    piece = jnp.where(core == 0, pair, moved)
-    block = exchange(jnp.broadcast_to(piece[None], (CHIPS, 2 * SLICE, D)), MIXED)
+    piece = jnp.where(core == 0, jnp.concatenate((singles, first)), jnp.concatenate((first, moved)))
+    pieces, held = lax.optimization_barrier((jnp.broadcast_to(piece[None], (CHIPS, 2 * SLICE, D)), singles))
+    wt_h, wt_l, wo_h, wo_l, gate = prepare(held, norm_gain, w_out, w_gate, w_query, w_key, w_value)
+    block = exchange(pieces, MIXED)
+    block, wt_h, wt_l, gate = lax.optimization_barrier((block, wt_h, wt_l, gate))
     swapped = lax.ppermute(block, AXES, SIBLING)
     message = attend(core, block, swapped, (wt_h, wt_l), stage(core, pair_bias, other))
     parts = exchange(message, OVER_M)

time: 67.5 us -> 66.1 us (0.979)
  waiting for transfers between devices: 9.66 us -> 5.97 us
  Pallas kernels: 9.18 us -> 11.3 us
  local copies, waits for them, and re-layouts: 1.53 us -> 0.82 us
    all_to_all x1, waiting for transfers between devices: 4.92 us -> 1.32 us  [exchange(): lax.all_to_all(pieces, AXES, 0, 0, tiled=True, axis_index_groups=groups)]
    ppermute x1, starting transfers between devices: 5.5 us -> 1.91 us  [body(): swapped = lax.ppermute(block, AXES, SIBLING)]
    all_to_all x1, starting transfers between devices: 6.66 us -> 9.56 us  [exchange(): lax.all_to_all(pieces, AXES, 0, 0, tiled=True, axis_index_groups=groups)]
    pallas_call x0 -> x1, Pallas kernels: none -> 2.22 us  [cut(): pl.pallas_call(cut_kernel, out_shape=pltpu.HBM(part, F32), in_specs=[pl.B...]
    ppermute x2, starting transfers between devices: 10.1 us -> 11 us  [the longest x1 8.91 us: body(): first = lax.ppermute(singles, AXES, TO_COLUMN_0)]
    unnamed x7 -> x8, local copies, waits for them, and re-layouts: 0.72 us -> 0.01 us
  transfers between devices with their start and end apart: 5 -> 5, of which waited for: 4 -> 4; matrix products, arithmetic and copies ran while one was open for 1% -> 0% of each run, Pallas kernels for 7% -> 10%
where the time goes in v5:
time: 66.1 us; the launch traced here: 65.6 us
  starting transfers between devices  24.4 us (37%)
  blocking collectives  23 us (35%)
  Pallas kernels  11.3 us (17%)
  waiting for transfers between devices  5.97 us (9%)
  local copies, waits for them, and re-layouts  0.82 us (1%)
    all_to_all x1, blocking collectives, exchange(): lax.all_to_all(pieces, AXES, 0, 0, tiled=True, axis_index_groups=groups)  23 us
    all_to_all x1, starting transfers between devices, exchange(): lax.all_to_all(pieces, AXES, 0, 0, tiled=True, axis_index_groups=groups)  9.56 us
    ppermute x1, starting transfers between devices, body(): first = lax.ppermute(singles, AXES, TO_COLUMN_0)  8.91 us
    ppermute x1, waiting for transfers between devices, body(): moved = lax.ppermute(singles, AXES, TO_COLUMN_1)  3.74 us
    pallas_call x1, Pallas kernels, attend(): pl.pallas_call(attend_kernel, out_shape=jax.ShapeDtypeStruct((CHIPS, SLIC...  3.52 us
    pallas_call x1, Pallas kernels, prepare(): pl.pallas_call(prepare_kernel, out_shape=[pltpu.VMEM((3 * D, D), BF16)] *...  3.3 us
    pallas_call x1, Pallas kernels, cut(): pl.pallas_call(cut_kernel, out_shape=pltpu.HBM(part, F32), in_specs=[pl.B...  2.22 us
    ppermute x1, starting transfers between devices, body(): moved = lax.ppermute(singles, AXES, TO_COLUMN_1)  2.08 us
  transfers between devices with their start and end apart: 5, of which 4 were waited for; matrix products, arithmetic and copies ran while one was open for 0% of the time, Pallas kernels for 10%

profile of v5, /device:TPU:1, one launch (start us, length us, event | category | flops | bytes accessed | tf_op | source)
XLA Modules:
  0.0 65.6 jit_solution(12808818002797547683)
XLA Ops:
  0.0 0.0 copy-start.2
  0.0 8.9 %collective-permute-start.1 = (f32[8,384]{1,0:T(8,128)}, f32[8,384]{1,0:T(8,128)S(1)}, u32[]{:S(2)}, u32[]{:S(2)}) collective-permute-start(f32[8,384]{1,0:T(8,128)} %singles.2), channel_id=1, source_target_pairs={{0,129},{2,385},{4,97},{6,353},{8,65},{10,321},{12,33},{14,289},{1... | collective-permute-start | bytes 36872 | tf_op jit(solution)/shard_map/ppermute | solution.py:292
  8.9 2.1 %collective-permute-start = (f32[8,384]{1,0:T(8,128)}, f32[8,384]{1,0:T(8,128)S(1)}, u32[]{:S(2)}, u32[]{:S(2)}) collective-permute-start(f32[8,384]{1,0:T(8,128)} %singles.2), channel_id=1, source_target_pairs={{1,129},{3,385},{5,97},{7,353},{9,65},{11,321},{13,33},{15,289},{1... | collective-permute-start | bytes 36872 | tf_op jit(solution)/shard_map/ppermute | solution.py:291
  11.0 2.2 %cut.1 = f32[16,16,8,128]{3,2,1,0:T(8,128)} custom-call(s32[1]{0:T(128)} %bitcast.core_ref, f32[16,16,2,8,128]{4,3,2,1,0:T(8,128)} %bitcast.6), custom_call_target="tpu_custom_call" | custom-call | bytes 4194304 | tf_op jit(solution)/shard_map/cut/pallas_call | solution.py:164
  13.2 0.5 collective-permute-done.1
  13.7 3.7 %collective-permute-done = f32[8,384]{1,0:T(8,128)S(1)} collective-permute-done((f32[8,384]{1,0:T(8,128)}, f32[8,384]{1,0:T(8,128)S(1)}, u32[]{:S(2)}, u32[]{:S(2)}) %collective-permute-start) | collective-permute-done | bytes 12320 | tf_op jit(solution)/shard_map/ppermute | solution.py:291
  17.5 0.0 copy-done.2
  17.5 0.8 %broadcast_in_dim.2 = f32[16,16,384]{2,1,0:T(8,128)} broadcast(f32[16,384]{1,0:T(8,128)S(1)} %maximum_select_fusion), dimensions={1,2} | broadcast | bytes 417792 | tf_op jit(solution)/shard_map/broadcast_in_dim | solution.py:297
  18.3 9.6 %all-to-all-start = ((f32[16,16,384]{2,1,0:T(8,128)}), f32[16,16,384]{2,1,0:T(8,128)S(1)}, u32[]{:S(2)}, u32[]{:S(2)}) async-start(f32[16,16,384]{2,1,0:T(8,128)} %broadcast_in_dim.2), calls=%async_computation | async-start | bytes 786432 | tf_op jit(solution)/shard_map/all_to_all | solution.py:59
  27.9 1.9 %collective-permute-start.3 = (f32[16,16,8,128]{3,2,1,0:T(8,128)}, f32[16,16,8,128]{3,2,1,0:T(8,128)S(1)}, u32[]{:S(2)}, u32[]{:S(2)}) collective-permute-start(f32[16,16,8,128]{3,2,1,0:T(8,128)} %cut.1), channel_id=1, source_target_pairs={{0,1},{1,0},{2,3},{3,2},{4,5},{5,4},{6,7},{7,6},{8,9},{9,8},{10,11... | collective-permute-start | bytes 3145736 | tf_op jit(solution)/shard_map/ppermute | solution.py:295
  29.8 3.3 %prepare.1 = (bf16[1152,384]{1,0:T(8,128)(2,1)S(1)}, bf16[1152,384]{1,0:T(8,128)(2,1)S(1)}, bf16[512,384]{1,0:T(8,128)(2,1)}, bf16[512,384]{1,0:T(8,128)(2,1)}, f32[8,512]{1,0:T(8,128)S(1)}) custom-call(f32[8,384]{1,0:T(8,128)} %singles.2, f32[384]{0:T(512)} %gain.1, f32[384,384]{1,0:T(8,128)} %w_out.1, f32[384,384]{1,0:T(8,128)} %w_gate.1, ...), custom_call_target="tpu_custom_call" | custom-call | flops 905969664 | bytes 8388608 | tf_op jit(solution)/shard_map/prepare/pallas_call | solution.py:140
  33.1 1.3 %all-to-all-done = f32[16,16,384]{2,1,0:T(8,128)S(1)} async-done(((f32[16,16,384]{2,1,0:T(8,128)}), f32[16,16,384]{2,1,0:T(8,128)S(1)}, u32[]{:S(2)}, u32[]{:S(2)}) %all-to-all-start) | async-done | bytes 393248 | tf_op jit(solution)/shard_map/all_to_all | solution.py:59
  34.4 1.9 %collective-permute-start.2 = (f32[16,16,384]{2,1,0:T(8,128)S(1)}, f32[16,16,384]{2,1,0:T(8,128)S(1)}, u32[]{:S(2)}, u32[]{:S(2)}) collective-permute-start(f32[16,16,384]{2,1,0:T(8,128)S(1)} %all-to-all-done), channel_id=1, source_target_pairs={{0,1},{1,0},{2,3},{3,2},{4,5},{5,4},{6,7},{7,6},{8,9},{9,8},{10,11... | collective-permute-start | bytes 1179656 | tf_op jit(solution)/shard_map/ppermute | solution.py:301
  36.3 0.0 collective-permute-done.3.other
  36.3 1.2 %stage.1.held = f32[2,16,16,8,128]{4,3,2,1,0:T(8,128)S(1)} custom-call(s32[1]{0:T(128)} %bitcast.core_ref, f32[16,16,2,8,128]{4,3,2,1,0:T(8,128)} %bitcast.7, f32[16,16,8,128]{3,2,1,0:T(8,128)S(1)} %collective-permute-done.3.other), custom_call_target="tpu_custom_call" | custom-call | bytes 4194304 | tf_op jit(solution)/shard_map/stage/pallas_call | solution.py:184
  37.6 0.4 collective-permute-done.2
  38.0 0.0 copy-start
  38.0 0.0 copy-start.1
  38.0 3.5 %attend.1 = f32[16,8,512]{2,1,0:T(8,128)S(1)} custom-call(s32[1]{0:T(128)} %bitcast.core_ref, f32[16,2,8,384]{3,2,1,0:T(8,128)S(1)} %bitcast.4, f32[16,2,8,384]{3,2,1,0:T(8,128)S(1)} %bitcast.5, bf16[1152,384]{1,0:T(8,128)(2,1)S(1)} %get-tuple-element.27.wt_h, bf16[1152,384]{1,0:T(8,128)(2,1)S(1)} %get-tuple-element.28.wt_l, ...), custom_call_target="tpu_custom_call" | custom-call | flops 1000000000 | bytes 6291456 | tf_op jit(solution)/shard_map/attend/pallas_call | solution.py:250
  41.5 23.0 %all_to_all.10.parts = f32[16,8,512]{2,1,0:T(8,128)S(1)} all-to-all(f32[16,8,512]{2,1,0:T(8,128)S(1)} %attend.1), channel_id=1, replica_groups={{0,2,4,6,8,10,12,14,16,18,20,22,24,26,28,30},{1,3,5,7,9,11,13,15,17,19,..., dimensions={0} | all-to-all | bytes 524288 | tf_op jit(solution)/shard_map/all_to_all | solution.py:59
  64.6 0.0 copy-done
  64.6 0.0 copy-done.1
  64.6 0.0 copy-done.3
  64.6 1.0 %finish.1 = f32[8,384]{1,0:T(8,128)} custom-call(f32[16,8,512]{2,1,0:T(8,128)S(1)} %all_to_all.10.parts, f32[8,512]{1,0:T(8,128)S(1)} %get-tuple-element.30.gate, bf16[512,384]{1,0:T(8,128)(2,1)S(1)} %copy-done, bf16[512,384]{1,0:T(8,128)(2,1)S(1)} %copy-done.1, f32[8,384]{1,0:T(8,128)S(1)} %copy-done.3), custom_call_target="tpu_custom_call" | custom-call | flops 9437184 | bytes 2097152 | tf_op jit(solution)/shard_map/finish/pallas_call | solution.py:280
  (2 shorter events, 0.0 us)
Async XLA Ops:
  0.0 17.5 %copy-start.2 = (f32[8,384]{1,0:T(8,128)S(1)}, f32[8,384]{1,0:T(8,128)}, u32[]{:S(2)}) copy-start(f32[8,384]{1,0:T(8,128)} %singles.2) | copy-start | bytes 36868
  0.0 13.7 %collective-permute-start.1 = (f32[8,384]{1,0:T(8,128)}, f32[8,384]{1,0:T(8,128)S(1)}, u32[]{:S(2)}, u32[]{:S(2)}) collective-permute-start(f32[8,384]{1,0:T(8,128)} %singles.2), channel_id=1, source_target_pairs={{0,129},{2,385},{4,97},{6,353},{8,65},{10,321},{12,33},{14,289},{1... | collective-permute-start | bytes 36872 | tf_op jit(solution)/shard_map/ppermute | solution.py:292
  8.9 8.6 %collective-permute-start = (f32[8,384]{1,0:T(8,128)}, f32[8,384]{1,0:T(8,128)S(1)}, u32[]{:S(2)}, u32[]{:S(2)}) collective-permute-start(f32[8,384]{1,0:T(8,128)} %singles.2), channel_id=1, source_target_pairs={{1,129},{3,385},{5,97},{7,353},{9,65},{11,321},{13,33},{15,289},{1... | collective-permute-start | bytes 36872 | tf_op jit(solution)/shard_map/ppermute | solution.py:291
  18.3 16.1 %all-to-all-start = ((f32[16,16,384]{2,1,0:T(8,128)}), f32[16,16,384]{2,1,0:T(8,128)S(1)}, u32[]{:S(2)}, u32[]{:S(2)}) async-start(f32[16,16,384]{2,1,0:T(8,128)} %broadcast_in_dim.2), calls=%async_computation | async-start | bytes 786432 | tf_op jit(solution)/shard_map/all_to_all | solution.py:59
  27.9 8.5 %collective-permute-start.3 = (f32[16,16,8,128]{3,2,1,0:T(8,128)}, f32[16,16,8,128]{3,2,1,0:T(8,128)S(1)}, u32[]{:S(2)}, u32[]{:S(2)}) collective-permute-start(f32[16,16,8,128]{3,2,1,0:T(8,128)} %cut.1), channel_id=1, source_target_pairs={{0,1},{1,0},{2,3},{3,2},{4,5},{5,4},{6,7},{7,6},{8,9},{9,8},{10,11... | collective-permute-start | bytes 3145736 | tf_op jit(solution)/shard_map/ppermute | solution.py:295
  34.4 3.6 %collective-permute-start.2 = (f32[16,16,384]{2,1,0:T(8,128)S(1)}, f32[16,16,384]{2,1,0:T(8,128)S(1)}, u32[]{:S(2)}, u32[]{:S(2)}) collective-permute-start(f32[16,16,384]{2,1,0:T(8,128)S(1)} %all-to-all-done), channel_id=1, source_target_pairs={{0,1},{1,0},{2,3},{3,2},{4,5},{5,4},{6,7},{7,6},{8,9},{9,8},{10,11... | collective-permute-start | bytes 1179656 | tf_op jit(solution)/shard_map/ppermute | solution.py:301
  38.0 26.6 %copy-start = (bf16[512,384]{1,0:T(8,128)(2,1)S(1)}, bf16[512,384]{1,0:T(8,128)(2,1)}, u32[]{:S(2)}) copy-start(bf16[512,384]{1,0:T(8,128)(2,1)} %get-tuple-element.31.wo_h) | copy-start | bytes 1179652
  38.0 26.6 %copy-start.1 = (bf16[512,384]{1,0:T(8,128)(2,1)S(1)}, bf16[512,384]{1,0:T(8,128)(2,1)}, u32[]{:S(2)}) copy-start(bf16[512,384]{1,0:T(8,128)(2,1)} %get-tuple-element.32.wo_l) | copy-start | bytes 1179652
  38.0 26.6 %copy-start.3 = (f32[8,384]{1,0:T(8,128)S(1)}, f32[8,384]{1,0:T(8,128)}, u32[]{:S(2)}) copy-start(f32[8,384]{1,0:T(8,128)} %singles.2) | copy-start | bytes 36868

commit v6 on v5

--- a/solution.py
+++ b/solution.py
@@ -35,11 +35,12 @@
 
 
 HOLDERS = [holders(m) for m in range(CHIPS)]
-OVER_M = [[r * COL + 2 * m + k for m in range(CHIPS)] for r in range(ROW) for k in range(2)]
+ALONG_Z = [2 * z + x for x in range(2) for z in range(8)]
+OVER_M = [[r * COL + 2 * m + k for m in ALONG_Z] for r in range(ROW) for k in range(2)]
 SIBLING = [(i, i ^ 1) for i in range(ROW * COL)]
 
 
-MIXED = [[r * COL + 2 * m for m in range(CHIPS)] for r in range(ROW)] + [
+MIXED = [[r * COL + 2 * m for m in ALONG_Z] for r in range(ROW)] + [
     [r * COL + 2 * m + 1 for r in HOLDERS[m]] for m in range(CHIPS)
 ]
 
@@ -175,7 +176,12 @@
 
 def stage_kernel(core_ref, bias, other, held, sems):
     core = core_ref[0]
-    for copy in fetch((bias.at[:, :, core], other), (held.at[core], held.at[1 - core]), sems):
+    sources, targets = [], []
+    for x in range(2):
+        chips = pl.ds(x * 8, 8)
+        sources += [bias.at[:, :, x, core], other.at[:, :, x]]
+        targets += [held.at[core, :, chips], held.at[1 - core, :, chips]]
+    for copy in fetch(sources, targets, sems):
         copy.wait()
 
 
@@ -186,11 +192,11 @@
         out_shape=pltpu.VMEM((2, HEADS, CHIPS, SLICE, LANES), F32),
         in_specs=[pl.BlockSpec(memory_space=pltpu.SMEM)] + [hbm] * 2,
         out_specs=pl.BlockSpec(memory_space=pltpu.VMEM),
-        scratch_shapes=[pltpu.SemaphoreType.DMA((2,))],
+        scratch_shapes=[pltpu.SemaphoreType.DMA((4,))],
         compiler_params=pltpu.CompilerParams(vmem_limit_bytes=20 << 20),
         cost_estimate=pl.CostEstimate(flops=0, bytes_accessed=4 << 20, transcendentals=0),
         name="stage",
-    )(core.reshape(1), *in_hbm(bias.reshape(HEADS, CHIPS, 2, SLICE, LANES)), other)
+    )(core.reshape(1), *in_hbm(bias.reshape(HEADS, 8, 2, 2, SLICE, LANES)), other.reshape(HEADS, 8, 2, SLICE, LANES))
 
 
 def attend_kernel(core_ref, block, swapped, wt_h, wt_l, held, out):

time: 66.1 us -> 63.8 us (0.965)
  blocking collectives: 23 us -> 20.8 us
    all_to_all x1, blocking collectives: 23 us -> 20.8 us  [exchange(): lax.all_to_all(pieces, AXES, 0, 0, tiled=True, axis_index_groups=groups)]
  transfers between devices with their start and end apart: 5 -> 5, of which waited for: 4 -> 4; matrix products, arithmetic and copies ran while one was open for 0% -> 0% of each run, Pallas kernels for 10% -> 11%
where the time goes in v6:
time: 63.8 us; the launch traced here: 63.4 us
  starting transfers between devices  24.4 us (38%)
  blocking collectives  20.8 us (33%)
  Pallas kernels  11.4 us (18%)
  waiting for transfers between devices  5.95 us (9%)
  local copies, waits for them, and re-layouts  0.82 us (1%)
    all_to_all x1, blocking collectives, exchange(): lax.all_to_all(pieces, AXES, 0, 0, tiled=True, axis_index_groups=groups)  20.8 us
    all_to_all x1, starting transfers between devices, exchange(): lax.all_to_all(pieces, AXES, 0, 0, tiled=True, axis_index_groups=groups)  9.56 us
    ppermute x1, starting transfers between devices, body(): first = lax.ppermute(singles, AXES, TO_COLUMN_0)  8.91 us
    ppermute x1, waiting for transfers between devices, body(): moved = lax.ppermute(singles, AXES, TO_COLUMN_1)  3.74 us
    pallas_call x1, Pallas kernels, attend(): pl.pallas_call(attend_kernel, out_shape=jax.ShapeDtypeStruct((CHIPS, SLIC...  3.52 us
    pallas_call x1, Pallas kernels, prepare(): pl.pallas_call(prepare_kernel, out_shape=[pltpu.VMEM((3 * D, D), BF16)] *...  3.3 us
    pallas_call x1, Pallas kernels, cut(): pl.pallas_call(cut_kernel, out_shape=pltpu.HBM(part, F32), in_specs=[pl.B...  2.22 us
    ppermute x1, starting transfers between devices, body(): moved = lax.ppermute(singles, AXES, TO_COLUMN_1)  2.08 us
  transfers between devices with their start and end apart: 5, of which 4 were waited for; matrix products, arithmetic and copies ran while one was open for 0% of the time, Pallas kernels for 11%

profile of v6, /device:TPU:1, one launch (start us, length us, event | category | flops | bytes accessed | tf_op | source)
XLA Modules:
  0.0 63.4 jit_solution(10832141011731516148)
XLA Ops:
  0.0 0.0 copy-start.2
  0.0 8.9 %collective-permute-start.1 = (f32[8,384]{1,0:T(8,128)}, f32[8,384]{1,0:T(8,128)S(1)}, u32[]{:S(2)}, u32[]{:S(2)}) collective-permute-start(f32[8,384]{1,0:T(8,128)} %singles.2), channel_id=1, source_target_pairs={{0,129},{2,385},{4,97},{6,353},{8,65},{10,321},{12,33},{14,289},{1... | collective-permute-start | bytes 36872 | tf_op jit(solution)/shard_map/ppermute | solution.py:298
  8.9 2.1 %collective-permute-start = (f32[8,384]{1,0:T(8,128)}, f32[8,384]{1,0:T(8,128)S(1)}, u32[]{:S(2)}, u32[]{:S(2)}) collective-permute-start(f32[8,384]{1,0:T(8,128)} %singles.2), channel_id=1, source_target_pairs={{1,129},{3,385},{5,97},{7,353},{9,65},{11,321},{13,33},{15,289},{1... | collective-permute-start | bytes 36872 | tf_op jit(solution)/shard_map/ppermute | solution.py:297
  11.0 2.2 %cut.1 = f32[16,16,8,128]{3,2,1,0:T(8,128)} custom-call(s32[1]{0:T(128)} %bitcast.core_ref, f32[16,16,2,8,128]{4,3,2,1,0:T(8,128)} %bitcast.9), custom_call_target="tpu_custom_call" | custom-call | bytes 4194304 | tf_op jit(solution)/shard_map/cut/pallas_call | solution.py:165
  13.2 0.5 collective-permute-done.1
  13.7 3.7 %collective-permute-done = f32[8,384]{1,0:T(8,128)S(1)} collective-permute-done((f32[8,384]{1,0:T(8,128)}, f32[8,384]{1,0:T(8,128)S(1)}, u32[]{:S(2)}, u32[]{:S(2)}) %collective-permute-start) | collective-permute-done | bytes 12320 | tf_op jit(solution)/shard_map/ppermute | solution.py:297
  17.5 0.0 copy-done.2
  17.5 0.8 %broadcast_in_dim.2 = f32[16,16,384]{2,1,0:T(8,128)} broadcast(f32[16,384]{1,0:T(8,128)S(1)} %maximum_select_fusion), dimensions={1,2} | broadcast | bytes 417792 | tf_op jit(solution)/shard_map/broadcast_in_dim | solution.py:303
  18.3 9.6 %all-to-all-start = ((f32[16,16,384]{2,1,0:T(8,128)}), f32[16,16,384]{2,1,0:T(8,128)S(1)}, u32[]{:S(2)}, u32[]{:S(2)}) async-start(f32[16,16,384]{2,1,0:T(8,128)} %broadcast_in_dim.2), calls=%async_computation | async-start | bytes 786432 | tf_op jit(solution)/shard_map/all_to_all | solution.py:60
  27.9 1.9 %collective-permute-start.3 = (f32[16,16,8,128]{3,2,1,0:T(8,128)}, f32[16,16,8,128]{3,2,1,0:T(8,128)S(1)}, u32[]{:S(2)}, u32[]{:S(2)}) collective-permute-start(f32[16,16,8,128]{3,2,1,0:T(8,128)} %cut.1), channel_id=1, source_target_pairs={{0,1},{1,0},{2,3},{3,2},{4,5},{5,4},{6,7},{7,6},{8,9},{9,8},{10,11... | collective-permute-start | bytes 3145736 | tf_op jit(solution)/shard_map/ppermute | solution.py:301
  29.8 3.3 %prepare.1 = (bf16[1152,384]{1,0:T(8,128)(2,1)S(1)}, bf16[1152,384]{1,0:T(8,128)(2,1)S(1)}, bf16[512,384]{1,0:T(8,128)(2,1)}, bf16[512,384]{1,0:T(8,128)(2,1)}, f32[8,512]{1,0:T(8,128)S(1)}) custom-call(f32[8,384]{1,0:T(8,128)} %singles.2, f32[384]{0:T(512)} %gain.1, f32[384,384]{1,0:T(8,128)} %w_out.1, f32[384,384]{1,0:T(8,128)} %w_gate.1, ...), custom_call_target="tpu_custom_call" | custom-call | flops 905969664 | bytes 8388608 | tf_op jit(solution)/shard_map/prepare/pallas_call | solution.py:141
  33.1 1.3 %all-to-all-done = f32[16,16,384]{2,1,0:T(8,128)S(1)} async-done(((f32[16,16,384]{2,1,0:T(8,128)}), f32[16,16,384]{2,1,0:T(8,128)S(1)}, u32[]{:S(2)}, u32[]{:S(2)}) %all-to-all-start) | async-done | bytes 393248 | tf_op jit(solution)/shard_map/all_to_all | solution.py:60
  34.4 1.9 %collective-permute-start.2 = (f32[16,16,384]{2,1,0:T(8,128)S(1)}, f32[16,16,384]{2,1,0:T(8,128)S(1)}, u32[]{:S(2)}, u32[]{:S(2)}) collective-permute-start(f32[16,16,384]{2,1,0:T(8,128)S(1)} %all-to-all-done), channel_id=1, source_target_pairs={{0,1},{1,0},{2,3},{3,2},{4,5},{5,4},{6,7},{7,6},{8,9},{9,8},{10,11... | collective-permute-start | bytes 1179656 | tf_op jit(solution)/shard_map/ppermute | solution.py:307
  36.3 0.0 collective-permute-done.3
  36.3 1.3 %stage.1.held = f32[2,16,16,8,128]{4,3,2,1,0:T(8,128)S(1)} custom-call(s32[1]{0:T(128)} %bitcast.core_ref, f32[16,8,2,2,8,128]{5,4,3,2,1,0:T(8,128)} %bitcast.10, f32[16,8,2,8,128]{4,3,2,1,0:T(8,128)S(1)} %bitcast.7), custom_call_target="tpu_custom_call" | custom-call | bytes 4194304 | tf_op jit(solution)/shard_map/stage/pallas_call | solution.py:190
  37.6 0.4 collective-permute-done.2
  38.0 0.0 copy-start
  38.0 0.0 copy-start.1
  38.0 3.5 %attend.1 = f32[16,8,512]{2,1,0:T(8,128)S(1)} custom-call(s32[1]{0:T(128)} %bitcast.core_ref, f32[16,2,8,384]{3,2,1,0:T(8,128)S(1)} %bitcast.6, f32[16,2,8,384]{3,2,1,0:T(8,128)S(1)} %bitcast.8, bf16[1152,384]{1,0:T(8,128)(2,1)S(1)} %get-tuple-element.27.wt_h, bf16[1152,384]{1,0:T(8,128)(2,1)S(1)} %get-tuple-element.28.wt_l, ...), custom_call_target="tpu_custom_call" | custom-call | flops 1000000000 | bytes 6291456 | tf_op jit(solution)/shard_map/attend/pallas_call | solution.py:256
  41.5 20.8 %all_to_all.10.parts = f32[16,8,512]{2,1,0:T(8,128)S(1)} all-to-all(f32[16,8,512]{2,1,0:T(8,128)S(1)} %attend.1), channel_id=1, replica_groups={{0,4,8,12,16,20,24,28,2,6,10,14,18,22,26,30},{1,5,9,13,17,21,25,29,3,7,..., dimensions={0} | all-to-all | bytes 524288 | tf_op jit(solution)/shard_map/all_to_all | solution.py:60
  62.3 0.0 copy-done
  62.3 0.0 copy-done.1
  62.3 0.0 copy-done.3
  62.3 1.0 %finish.1 = f32[8,384]{1,0:T(8,128)} custom-call(f32[16,8,512]{2,1,0:T(8,128)S(1)} %all_to_all.10.parts, f32[8,512]{1,0:T(8,128)S(1)} %get-tuple-element.30.gate, bf16[512,384]{1,0:T(8,128)(2,1)S(1)} %copy-done, bf16[512,384]{1,0:T(8,128)(2,1)S(1)} %copy-done.1, f32[8,384]{1,0:T(8,128)S(1)} %copy-done.3), custom_call_target="tpu_custom_call" | custom-call | flops 9437184 | bytes 2097152 | tf_op jit(solution)/shard_map/finish/pallas_call | solution.py:286
  (2 shorter events, 0.0 us)
Async XLA Ops:
  0.0 17.5 %copy-start.2 = (f32[8,384]{1,0:T(8,128)S(1)}, f32[8,384]{1,0:T(8,128)}, u32[]{:S(2)}) copy-start(f32[8,384]{1,0:T(8,128)} %singles.2) | copy-start | bytes 36868
  0.0 13.7 %collective-permute-start.1 = (f32[8,384]{1,0:T(8,128)}, f32[8,384]{1,0:T(8,128)S(1)}, u32[]{:S(2)}, u32[]{:S(2)}) collective-permute-start(f32[8,384]{1,0:T(8,128)} %singles.2), channel_id=1, source_target_pairs={{0,129},{2,385},{4,97},{6,353},{8,65},{10,321},{12,33},{14,289},{1... | collective-permute-start | bytes 36872 | tf_op jit(solution)/shard_map/ppermute | solution.py:298
  8.9 8.6 %collective-permute-start = (f32[8,384]{1,0:T(8,128)}, f32[8,384]{1,0:T(8,128)S(1)}, u32[]{:S(2)}, u32[]{:S(2)}) collective-permute-start(f32[8,384]{1,0:T(8,128)} %singles.2), channel_id=1, source_target_pairs={{1,129},{3,385},{5,97},{7,353},{9,65},{11,321},{13,33},{15,289},{1... | collective-permute-start | bytes 36872 | tf_op jit(solution)/shard_map/ppermute | solution.py:297
  18.3 16.1 %all-to-all-start = ((f32[16,16,384]{2,1,0:T(8,128)}), f32[16,16,384]{2,1,0:T(8,128)S(1)}, u32[]{:S(2)}, u32[]{:S(2)}) async-start(f32[16,16,384]{2,1,0:T(8,128)} %broadcast_in_dim.2), calls=%async_computation | async-start | bytes 786432 | tf_op jit(solution)/shard_map/all_to_all | solution.py:60
  27.9 8.5 %collective-permute-start.3 = (f32[16,16,8,128]{3,2,1,0:T(8,128)}, f32[16,16,8,128]{3,2,1,0:T(8,128)S(1)}, u32[]{:S(2)}, u32[]{:S(2)}) collective-permute-start(f32[16,16,8,128]{3,2,1,0:T(8,128)} %cut.1), channel_id=1, source_target_pairs={{0,1},{1,0},{2,3},{3,2},{4,5},{5,4},{6,7},{7,6},{8,9},{9,8},{10,11... | collective-permute-start | bytes 3145736 | tf_op jit(solution)/shard_map/ppermute | solution.py:301
  34.4 3.6 %collective-permute-start.2 = (f32[16,16,384]{2,1,0:T(8,128)S(1)}, f32[16,16,384]{2,1,0:T(8,128)S(1)}, u32[]{:S(2)}, u32[]{:S(2)}) collective-permute-start(f32[16,16,384]{2,1,0:T(8,128)S(1)} %all-to-all-done), channel_id=1, source_target_pairs={{0,1},{1,0},{2,3},{3,2},{4,5},{5,4},{6,7},{7,6},{8,9},{9,8},{10,11... | collective-permute-start | bytes 1179656 | tf_op jit(solution)/shard_map/ppermute | solution.py:307
  38.0 24.3 %copy-start = (bf16[512,384]{1,0:T(8,128)(2,1)S(1)}, bf16[512,384]{1,0:T(8,128)(2,1)}, u32[]{:S(2)}) copy-start(bf16[512,384]{1,0:T(8,128)(2,1)} %get-tuple-element.31.wo_h) | copy-start | bytes 1179652
  38.0 24.3 %copy-start.1 = (bf16[512,384]{1,0:T(8,128)(2,1)S(1)}, bf16[512,384]{1,0:T(8,128)(2,1)}, u32[]{:S(2)}) copy-start(bf16[512,384]{1,0:T(8,128)(2,1)} %get-tuple-element.32.wo_l) | copy-start | bytes 1179652
  38.0 24.3 %copy-start.3 = (f32[8,384]{1,0:T(8,128)S(1)}, f32[8,384]{1,0:T(8,128)}, u32[]{:S(2)}) copy-start(f32[8,384]{1,0:T(8,128)} %singles.2) | copy-start | bytes 36868

commit v7 on v6

--- a/solution.py
+++ b/solution.py
@@ -153,9 +153,13 @@
 
 
 def cut_kernel(core_ref, bias, theirs, half, sems):
-    for copy in fetch((bias.at[:, :, 1 - core_ref[0]],), (half,), sems):
+    parts = [pl.ds(i * GROUP, GROUP) for i in range(GROUPS)]
+    ins = fetch([bias.at[p, :, 1 - core_ref[0]] for p in parts], [half.at[p] for p in parts], sems)
+    outs = []
+    for i, copy in enumerate(ins):
         copy.wait()
-    for copy in fetch((half,), (theirs,), sems.at[pl.ds(1, 1)]):
+        outs += fetch((half.at[parts[i]],), (theirs.at[parts[i]],), sems.at[pl.ds(GROUPS + i, 1)])
+    for copy in outs:
         copy.wait()
 
 
@@ -167,7 +171,7 @@
         out_shape=pltpu.HBM(part, F32),
         in_specs=[pl.BlockSpec(memory_space=pltpu.SMEM), hbm],
         out_specs=hbm,
-        scratch_shapes=[pltpu.VMEM(part, F32), pltpu.SemaphoreType.DMA((2,))],
+        scratch_shapes=[pltpu.VMEM(part, F32), pltpu.SemaphoreType.DMA((2 * GROUPS,))],
         compiler_params=pltpu.CompilerParams(vmem_limit_bytes=20 << 20),
         cost_estimate=pl.CostEstimate(flops=0, bytes_accessed=4 << 20, transcendentals=0),
         name="cut",

time: 63.8 us -> 63.8 us (level)
  transfers between devices with their start and end apart: 5 -> 5, of which waited for: 4 -> 4; matrix products, arithmetic and copies ran while one was open for 0% -> 0% of each run, Pallas kernels for 11% -> 10%
where the time goes in v7:
time: 63.8 us; the launch traced here: 63.4 us
  starting transfers between devices  24.1 us (38%)
  blocking collectives  21 us (33%)
  Pallas kernels  11.1 us (17%)
  waiting for transfers between devices  6.17 us (10%)
  local copies, waits for them, and re-layouts  0.82 us (1%)
    all_to_all x1, blocking collectives, exchange(): lax.all_to_all(pieces, AXES, 0, 0, tiled=True, axis_index_groups=groups)  21 us
    all_to_all x1, starting transfers between devices, exchange(): lax.all_to_all(pieces, AXES, 0, 0, tiled=True, axis_index_groups=groups)  9.34 us
    ppermute x1, starting transfers between devices, body(): first = lax.ppermute(singles, AXES, TO_COLUMN_0)  8.91 us
    ppermute x1, waiting for transfers between devices, body(): moved = lax.ppermute(singles, AXES, TO_COLUMN_1)  3.74 us
    pallas_call x1, Pallas kernels, attend(): pl.pallas_call(attend_kernel, out_shape=jax.ShapeDtypeStruct((CHIPS, SLIC...  3.52 us
    pallas_call x1, Pallas kernels, prepare(): pl.pallas_call(prepare_kernel, out_shape=[pltpu.VMEM((3 * D, D), BF16)] *...  3.3 us
    ppermute x1, starting transfers between devices, body(): moved = lax.ppermute(singles, AXES, TO_COLUMN_1)  2.08 us
    pallas_call x1, Pallas kernels, cut(): pl.pallas_call(cut_kernel, out_shape=pltpu.HBM(part, F32), in_specs=[pl.B...  2 us
  transfers between devices with their start and end apart: 5, of which 4 were waited for; matrix products, arithmetic and copies ran while one was open for 0% of the time, Pallas kernels for 10%

profile of v7, /device:TPU:1, one launch (start us, length us, event | category | flops | bytes accessed | tf_op | source)
XLA Modules:
  0.0 63.4 jit_solution(10453877648883753835)
XLA Ops:
  0.0 0.0 copy-start.2
  0.0 8.9 %collective-permute-start.1 = (f32[8,384]{1,0:T(8,128)}, f32[8,384]{1,0:T(8,128)S(1)}, u32[]{:S(2)}, u32[]{:S(2)}) collective-permute-start(f32[8,384]{1,0:T(8,128)} %singles.2), channel_id=1, source_target_pairs={{0,129},{2,385},{4,97},{6,353},{8,65},{10,321},{12,33},{14,289},{1... | collective-permute-start | bytes 36872 | tf_op jit(solution)/shard_map/ppermute | solution.py:302
  8.9 2.1 %collective-permute-start = (f32[8,384]{1,0:T(8,128)}, f32[8,384]{1,0:T(8,128)S(1)}, u32[]{:S(2)}, u32[]{:S(2)}) collective-permute-start(f32[8,384]{1,0:T(8,128)} %singles.2), channel_id=1, source_target_pairs={{1,129},{3,385},{5,97},{7,353},{9,65},{11,321},{13,33},{15,289},{1... | collective-permute-start | bytes 36872 | tf_op jit(solution)/shard_map/ppermute | solution.py:301
  11.0 2.0 %cut.1 = f32[16,16,8,128]{3,2,1,0:T(8,128)} custom-call(s32[1]{0:T(128)} %bitcast.core_ref, f32[16,16,2,8,128]{4,3,2,1,0:T(8,128)} %bitcast.9), custom_call_target="tpu_custom_call" | custom-call | bytes 4194304 | tf_op jit(solution)/shard_map/cut/pallas_call | solution.py:169
  13.0 0.7 %collective-permute-done.1 = f32[8,384]{1,0:T(8,128)S(1)} collective-permute-done((f32[8,384]{1,0:T(8,128)}, f32[8,384]{1,0:T(8,128)S(1)}, u32[]{:S(2)}, u32[]{:S(2)}) %collective-permute-start.1) | collective-permute-done | bytes 12320 | tf_op jit(solution)/shard_map/ppermute | solution.py:302
  13.7 3.7 %collective-permute-done = f32[8,384]{1,0:T(8,128)S(1)} collective-permute-done((f32[8,384]{1,0:T(8,128)}, f32[8,384]{1,0:T(8,128)S(1)}, u32[]{:S(2)}, u32[]{:S(2)}) %collective-permute-start) | collective-permute-done | bytes 12320 | tf_op jit(solution)/shard_map/ppermute | solution.py:301
  17.5 0.0 copy-done.2
  17.5 0.8 %broadcast_in_dim.2 = f32[16,16,384]{2,1,0:T(8,128)} broadcast(f32[16,384]{1,0:T(8,128)S(1)} %maximum_select_fusion), dimensions={1,2} | broadcast | bytes 417792 | tf_op jit(solution)/shard_map/broadcast_in_dim | solution.py:307
  18.3 9.3 %all-to-all-start = ((f32[16,16,384]{2,1,0:T(8,128)}), f32[16,16,384]{2,1,0:T(8,128)S(1)}, u32[]{:S(2)}, u32[]{:S(2)}) async-start(f32[16,16,384]{2,1,0:T(8,128)} %broadcast_in_dim.2), calls=%async_computation | async-start | bytes 786432 | tf_op jit(solution)/shard_map/all_to_all | solution.py:60
  27.6 1.9 %collective-permute-start.3 = (f32[16,16,8,128]{3,2,1,0:T(8,128)}, f32[16,16,8,128]{3,2,1,0:T(8,128)S(1)}, u32[]{:S(2)}, u32[]{:S(2)}) collective-permute-start(f32[16,16,8,128]{3,2,1,0:T(8,128)} %cut.1), channel_id=1, source_target_pairs={{0,1},{1,0},{2,3},{3,2},{4,5},{5,4},{6,7},{7,6},{8,9},{9,8},{10,11... | collective-permute-start | bytes 3145736 | tf_op jit(solution)/shard_map/ppermute | solution.py:305
  29.6 3.3 %prepare.1 = (bf16[1152,384]{1,0:T(8,128)(2,1)S(1)}, bf16[1152,384]{1,0:T(8,128)(2,1)S(1)}, bf16[512,384]{1,0:T(8,128)(2,1)}, bf16[512,384]{1,0:T(8,128)(2,1)}, f32[8,512]{1,0:T(8,128)S(1)}) custom-call(f32[8,384]{1,0:T(8,128)} %singles.2, f32[384]{0:T(512)} %gain.1, f32[384,384]{1,0:T(8,128)} %w_out.1, f32[384,384]{1,0:T(8,128)} %w_gate.1, ...), custom_call_target="tpu_custom_call" | custom-call | flops 905969664 | bytes 8388608 | tf_op jit(solution)/shard_map/prepare/pallas_call | solution.py:141
  32.9 1.3 %all-to-all-done = f32[16,16,384]{2,1,0:T(8,128)S(1)} async-done(((f32[16,16,384]{2,1,0:T(8,128)}), f32[16,16,384]{2,1,0:T(8,128)S(1)}, u32[]{:S(2)}, u32[]{:S(2)}) %all-to-all-start) | async-done | bytes 393248 | tf_op jit(solution)/shard_map/all_to_all | solution.py:60
  34.2 1.9 %collective-permute-start.2 = (f32[16,16,384]{2,1,0:T(8,128)S(1)}, f32[16,16,384]{2,1,0:T(8,128)S(1)}, u32[]{:S(2)}, u32[]{:S(2)}) collective-permute-start(f32[16,16,384]{2,1,0:T(8,128)S(1)} %all-to-all-done), channel_id=1, source_target_pairs={{0,1},{1,0},{2,3},{3,2},{4,5},{5,4},{6,7},{7,6},{8,9},{9,8},{10,11... | collective-permute-start | bytes 1179656 | tf_op jit(solution)/shard_map/ppermute | solution.py:311
  36.1 0.0 collective-permute-done.3
  36.1 1.3 %stage.1.held = f32[2,16,16,8,128]{4,3,2,1,0:T(8,128)S(1)} custom-call(s32[1]{0:T(128)} %bitcast.core_ref, f32[16,8,2,2,8,128]{5,4,3,2,1,0:T(8,128)} %bitcast.10, f32[16,8,2,8,128]{4,3,2,1,0:T(8,128)S(1)} %bitcast.7), custom_call_target="tpu_custom_call" | custom-call | bytes 4194304 | tf_op jit(solution)/shard_map/stage/pallas_call | solution.py:194
  37.4 0.4 collective-permute-done.2
  37.8 0.0 copy-start
  37.8 0.0 copy-start.1
  37.8 3.5 %attend.1 = f32[16,8,512]{2,1,0:T(8,128)S(1)} custom-call(s32[1]{0:T(128)} %bitcast.core_ref, f32[16,2,8,384]{3,2,1,0:T(8,128)S(1)} %bitcast.6, f32[16,2,8,384]{3,2,1,0:T(8,128)S(1)} %bitcast.8, bf16[1152,384]{1,0:T(8,128)(2,1)S(1)} %get-tuple-element.27.wt_h, bf16[1152,384]{1,0:T(8,128)(2,1)S(1)} %get-tuple-element.28.wt_l, ...), custom_call_target="tpu_custom_call" | custom-call | flops 1000000000 | bytes 6291456 | tf_op jit(solution)/shard_map/attend/pallas_call | solution.py:260
  41.3 21.0 %all_to_all.10.parts = f32[16,8,512]{2,1,0:T(8,128)S(1)} all-to-all(f32[16,8,512]{2,1,0:T(8,128)S(1)} %attend.1), channel_id=1, replica_groups={{0,4,8,12,16,20,24,28,2,6,10,14,18,22,26,30},{1,5,9,13,17,21,25,29,3,7,..., dimensions={0} | all-to-all | bytes 524288 | tf_op jit(solution)/shard_map/all_to_all | solution.py:60
  62.3 0.0 copy-done
  62.3 0.0 copy-done.1
  62.3 0.0 copy-done.3
  62.3 1.0 %finish.1 = f32[8,384]{1,0:T(8,128)} custom-call(f32[16,8,512]{2,1,0:T(8,128)S(1)} %all_to_all.10.parts, f32[8,512]{1,0:T(8,128)S(1)} %get-tuple-element.30.gate, bf16[512,384]{1,0:T(8,128)(2,1)S(1)} %copy-done, bf16[512,384]{1,0:T(8,128)(2,1)S(1)} %copy-done.1, f32[8,384]{1,0:T(8,128)S(1)} %copy-done.3), custom_call_target="tpu_custom_call" | custom-call | flops 9437184 | bytes 2097152 | tf_op jit(solution)/shard_map/finish/pallas_call | solution.py:290
  (2 shorter events, 0.0 us)
Async XLA Ops:
  0.0 17.5 %copy-start.2 = (f32[8,384]{1,0:T(8,128)S(1)}, f32[8,384]{1,0:T(8,128)}, u32[]{:S(2)}) copy-start(f32[8,384]{1,0:T(8,128)} %singles.2) | copy-start | bytes 36868
  0.0 13.7 %collective-permute-start.1 = (f32[8,384]{1,0:T(8,128)}, f32[8,384]{1,0:T(8,128)S(1)}, u32[]{:S(2)}, u32[]{:S(2)}) collective-permute-start(f32[8,384]{1,0:T(8,128)} %singles.2), channel_id=1, source_target_pairs={{0,129},{2,385},{4,97},{6,353},{8,65},{10,321},{12,33},{14,289},{1... | collective-permute-start | bytes 36872 | tf_op jit(solution)/shard_map/ppermute | solution.py:302
  8.9 8.6 %collective-permute-start = (f32[8,384]{1,0:T(8,128)}, f32[8,384]{1,0:T(8,128)S(1)}, u32[]{:S(2)}, u32[]{:S(2)}) collective-permute-start(f32[8,384]{1,0:T(8,128)} %singles.2), channel_id=1, source_target_pairs={{1,129},{3,385},{5,97},{7,353},{9,65},{11,321},{13,33},{15,289},{1... | collective-permute-start | bytes 36872 | tf_op jit(solution)/shard_map/ppermute | solution.py:301
  18.3 15.9 %all-to-all-start = ((f32[16,16,384]{2,1,0:T(8,128)}), f32[16,16,384]{2,1,0:T(8,128)S(1)}, u32[]{:S(2)}, u32[]{:S(2)}) async-start(f32[16,16,384]{2,1,0:T(8,128)} %broadcast_in_dim.2), calls=%async_computation | async-start | bytes 786432 | tf_op jit(solution)/shard_map/all_to_all | solution.py:60
  27.6 8.5 %collective-permute-start.3 = (f32[16,16,8,128]{3,2,1,0:T(8,128)}, f32[16,16,8,128]{3,2,1,0:T(8,128)S(1)}, u32[]{:S(2)}, u32[]{:S(2)}) collective-permute-start(f32[16,16,8,128]{3,2,1,0:T(8,128)} %cut.1), channel_id=1, source_target_pairs={{0,1},{1,0},{2,3},{3,2},{4,5},{5,4},{6,7},{7,6},{8,9},{9,8},{10,11... | collective-permute-start | bytes 3145736 | tf_op jit(solution)/shard_map/ppermute | solution.py:305
  34.2 3.6 %collective-permute-start.2 = (f32[16,16,384]{2,1,0:T(8,128)S(1)}, f32[16,16,384]{2,1,0:T(8,128)S(1)}, u32[]{:S(2)}, u32[]{:S(2)}) collective-permute-start(f32[16,16,384]{2,1,0:T(8,128)S(1)} %all-to-all-done), channel_id=1, source_target_pairs={{0,1},{1,0},{2,3},{3,2},{4,5},{5,4},{6,7},{7,6},{8,9},{9,8},{10,11... | collective-permute-start | bytes 1179656 | tf_op jit(solution)/shard_map/ppermute | solution.py:311
  37.8 24.6 %copy-start = (bf16[512,384]{1,0:T(8,128)(2,1)S(1)}, bf16[512,384]{1,0:T(8,128)(2,1)}, u32[]{:S(2)}) copy-start(bf16[512,384]{1,0:T(8,128)(2,1)} %get-tuple-element.31.wo_h) | copy-start | bytes 1179652
  37.8 24.6 %copy-start.1 = (bf16[512,384]{1,0:T(8,128)(2,1)S(1)}, bf16[512,384]{1,0:T(8,128)(2,1)}, u32[]{:S(2)}) copy-start(bf16[512,384]{1,0:T(8,128)(2,1)} %get-tuple-element.32.wo_l) | copy-start | bytes 1179652
  37.8 24.6 %copy-start.3 = (f32[8,384]{1,0:T(8,128)S(1)}, f32[8,384]{1,0:T(8,128)}, u32[]{:S(2)}) copy-start(f32[8,384]{1,0:T(8,128)} %singles.2) | copy-start | bytes 36868

commit v8 on v7

--- a/solution.py
+++ b/solution.py
@@ -301,7 +301,6 @@
     moved = lax.ppermute(singles, AXES, TO_COLUMN_1)
     first = lax.ppermute(singles, AXES, TO_COLUMN_0)
     theirs = cut(core, pair_bias)
-    moved, first, theirs = lax.optimization_barrier((moved, first, theirs))
     other = lax.ppermute(theirs, AXES, SIBLING)
     piece = jnp.where(core == 0, jnp.concatenate((singles, first)), jnp.concatenate((first, moved)))
     pieces, held = lax.optimization_barrier((jnp.broadcast_to(piece[None], (CHIPS, 2 * SLICE, D)), singles))

time: 63.8 us -> 66.7 us (1.045)
  starting transfers between devices: 24.1 us -> 30.4 us
  blocking collectives: 21 us -> 15.9 us
  waiting for transfers between devices: 6.17 us -> 7.23 us
  other arithmetic: 0.01 us -> 0.71 us
    ppermute x1, starting transfers between devices: 8.91 us -> 1.92 us  [body(): first = lax.ppermute(singles, AXES, TO_COLUMN_0)]
    all_to_all x1, starting transfers between devices: 9.34 us -> 15.9 us  [exchange(): lax.all_to_all(pieces, AXES, 0, 0, tiled=True, axis_index_groups=groups)]
    ppermute x1, starting transfers between devices: 2.08 us -> 8.27 us  [body(): moved = lax.ppermute(singles, AXES, TO_COLUMN_1)]
    all_to_all x1, blocking collectives: 21 us -> 15.9 us  [exchange(): lax.all_to_all(pieces, AXES, 0, 0, tiled=True, axis_index_groups=groups)]
    ppermute x1, waiting for transfers between devices: 0.71 us -> 4.67 us  [body(): first = lax.ppermute(singles, AXES, TO_COLUMN_0)]
    all_to_all x1, waiting for transfers between devices: 1.32 us -> 0.01 us  [exchange(): lax.all_to_all(pieces, AXES, 0, 0, tiled=True, axis_index_groups=groups)]
    ppermute x1, waiting for transfers between devices: 3.74 us -> 2.52 us  [body(): moved = lax.ppermute(singles, AXES, TO_COLUMN_1)]
    select_n x1, other arithmetic: 0.01 us -> 0.71 us  [body(): jnp.where(core == 0, jnp.concatenate((singles, first)), jnp.concatenate((...]
  transfers between devices with their start and end apart: 5 -> 5, of which waited for: 4 -> 2; matrix products, arithmetic and copies ran while one was open for 0% -> 0% of each run, Pallas kernels for 10% -> 10%
where the time goes in v8:
time: 66.7 us; the launch traced here: 66.2 us
  starting transfers between devices  30.4 us (46%)
  blocking collectives  15.9 us (24%)
  Pallas kernels  11.1 us (17%)
  waiting for transfers between devices  7.23 us (11%)
  local copies, waits for them, and re-layouts  0.8 us (1%)
  other arithmetic  0.71 us (1%)
    all_to_all x1, blocking collectives, exchange(): lax.all_to_all(pieces, AXES, 0, 0, tiled=True, axis_index_groups=groups)  15.9 us
    all_to_all x1, starting transfers between devices, exchange(): lax.all_to_all(pieces, AXES, 0, 0, tiled=True, axis_index_groups=groups)  15.9 us
    ppermute x1, starting transfers between devices, body(): moved = lax.ppermute(singles, AXES, TO_COLUMN_1)  8.27 us
    ppermute x1, waiting for transfers between devices, body(): first = lax.ppermute(singles, AXES, TO_COLUMN_0)  4.67 us
    pallas_call x1, Pallas kernels, attend(): pl.pallas_call(attend_kernel, out_shape=jax.ShapeDtypeStruct((CHIPS, SLIC...  3.51 us
    pallas_call x1, Pallas kernels, prepare(): pl.pallas_call(prepare_kernel, out_shape=[pltpu.VMEM((3 * D, D), BF16)] *...  3.3 us
    ppermute x1, waiting for transfers between devices, body(): moved = lax.ppermute(singles, AXES, TO_COLUMN_1)  2.52 us
    ppermute x1, starting transfers between devices, body(): swapped = lax.ppermute(block, AXES, SIBLING)  2.41 us
  transfers between devices with their start and end apart: 5, of which 2 were waited for; matrix products, arithmetic and copies ran while one was open for 0% of the time, Pallas kernels for 10%

profile of v8, /device:TPU:1, one launch (start us, length us, event | category | flops | bytes accessed | tf_op | source)
XLA Modules:
  0.0 66.2 jit_solution(9778311508265639909)
XLA Ops:
  0.0 8.3 %collective-permute-start.1 = (f32[8,384]{1,0:T(8,128)}, f32[8,384]{1,0:T(8,128)S(1)}, u32[]{:S(2)}, u32[]{:S(2)}) collective-permute-start(f32[8,384]{1,0:T(8,128)} %singles.2), channel_id=1, source_target_pairs={{1,129},{3,385},{5,97},{7,353},{9,65},{11,321},{13,33},{15,289},{1... | collective-permute-start | bytes 36872 | tf_op jit(solution)/shard_map/ppermute | solution.py:301
  8.3 1.9 %collective-permute-start = (f32[8,384]{1,0:T(8,128)}, f32[8,384]{1,0:T(8,128)S(1)}, u32[]{:S(2)}, u32[]{:S(2)}) collective-permute-start(f32[8,384]{1,0:T(8,128)} %singles.2), channel_id=1, source_target_pairs={{0,129},{2,385},{4,97},{6,353},{8,65},{10,321},{12,33},{14,289},{1... | collective-permute-start | bytes 36872 | tf_op jit(solution)/shard_map/ppermute | solution.py:302
  10.2 2.5 %collective-permute-done.1 = f32[8,384]{1,0:T(8,128)S(1)} collective-permute-done((f32[8,384]{1,0:T(8,128)}, f32[8,384]{1,0:T(8,128)S(1)}, u32[]{:S(2)}, u32[]{:S(2)}) %collective-permute-start.1) | collective-permute-done | bytes 12320 | tf_op jit(solution)/shard_map/ppermute | solution.py:301
  12.7 4.7 %collective-permute-done = f32[8,384]{1,0:T(8,128)S(1)} collective-permute-done((f32[8,384]{1,0:T(8,128)}, f32[8,384]{1,0:T(8,128)S(1)}, u32[]{:S(2)}, u32[]{:S(2)}) %collective-permute-start) | collective-permute-done | bytes 12320 | tf_op jit(solution)/shard_map/ppermute | solution.py:302
  17.4 0.7 %maximum_select_fusion = f32[16,384]{1,0:T(8,128)S(1)} fusion(f32[8,384]{1,0:T(8,128)S(1)} %collective-permute-done, f32[8,384]{1,0:T(8,128)} %singles.2, f32[8,384]{1,0:T(8,128)S(1)} %collective-permute-done.1, pred[]{:T(512)S(6)} %eq.5), kind=kLoop, calls=%fused_computation | loop fusion | flops 18432 | bytes 61441 | tf_op jit(solution)/shard_map/jit(_where)/select_n | solution.py:305
  18.1 0.8 %broadcast_in_dim.2 = f32[16,16,384]{2,1,0:T(8,128)} broadcast(f32[16,384]{1,0:T(8,128)S(1)} %maximum_select_fusion), dimensions={1,2} | broadcast | bytes 417792 | tf_op jit(solution)/shard_map/broadcast_in_dim | solution.py:306
  18.9 15.9 %all-to-all-start = ((f32[16,16,384]{2,1,0:T(8,128)}), f32[16,16,384]{2,1,0:T(8,128)S(1)}, u32[]{:S(2)}, u32[]{:S(2)}) async-start(f32[16,16,384]{2,1,0:T(8,128)} %broadcast_in_dim.2), calls=%async_computation | async-start | bytes 786432 | tf_op jit(solution)/shard_map/all_to_all | solution.py:60
  34.8 2.0 %cut.1 = f32[16,16,8,128]{3,2,1,0:T(8,128)} custom-call(s32[1]{0:T(128)} %bitcast.core_ref, f32[16,16,2,8,128]{4,3,2,1,0:T(8,128)} %bitcast.9), custom_call_target="tpu_custom_call" | custom-call | bytes 4194304 | tf_op jit(solution)/shard_map/cut/pallas_call | solution.py:169
  36.8 1.9 %collective-permute-start.3 = (f32[16,16,8,128]{3,2,1,0:T(8,128)}, f32[16,16,8,128]{3,2,1,0:T(8,128)S(1)}, u32[]{:S(2)}, u32[]{:S(2)}) collective-permute-start(f32[16,16,8,128]{3,2,1,0:T(8,128)} %cut.1), channel_id=1, source_target_pairs={{0,1},{1,0},{2,3},{3,2},{4,5},{5,4},{6,7},{7,6},{8,9},{9,8},{10,11... | collective-permute-start | bytes 3145736 | tf_op jit(solution)/shard_map/ppermute | solution.py:304
  38.7 3.3 %prepare.1 = (bf16[1152,384]{1,0:T(8,128)(2,1)S(1)}, bf16[1152,384]{1,0:T(8,128)(2,1)S(1)}, bf16[512,384]{1,0:T(8,128)(2,1)}, bf16[512,384]{1,0:T(8,128)(2,1)}, f32[8,512]{1,0:T(8,128)S(1)}) custom-call(f32[8,384]{1,0:T(8,128)} %singles.2, f32[384]{0:T(512)} %gain.1, f32[384,384]{1,0:T(8,128)} %w_out.1, f32[384,384]{1,0:T(8,128)} %w_gate.1, ...), custom_call_target="tpu_custom_call" | custom-call | flops 905969664 | bytes 8388608 | tf_op jit(solution)/shard_map/prepare/pallas_call | solution.py:141
  42.0 0.0 all-to-all-done
  42.0 2.4 %collective-permute-start.2 = (f32[16,16,384]{2,1,0:T(8,128)S(1)}, f32[16,16,384]{2,1,0:T(8,128)S(1)}, u32[]{:S(2)}, u32[]{:S(2)}) collective-permute-start(f32[16,16,384]{2,1,0:T(8,128)S(1)} %all-to-all-done), channel_id=1, source_target_pairs={{0,1},{1,0},{2,3},{3,2},{4,5},{5,4},{6,7},{7,6},{8,9},{9,8},{10,11... | collective-permute-start | bytes 1179656 | tf_op jit(solution)/shard_map/ppermute | solution.py:310
  44.4 0.0 collective-permute-done.3
  44.4 1.3 %stage.1.held = f32[2,16,16,8,128]{4,3,2,1,0:T(8,128)S(1)} custom-call(s32[1]{0:T(128)} %bitcast.core_ref, f32[16,8,2,2,8,128]{5,4,3,2,1,0:T(8,128)} %bitcast.10, f32[16,8,2,8,128]{4,3,2,1,0:T(8,128)S(1)} %bitcast.7), custom_call_target="tpu_custom_call" | custom-call | bytes 4194304 | tf_op jit(solution)/shard_map/stage/pallas_call | solution.py:194
  45.7 0.0 collective-permute-done.2
  45.8 0.0 copy-start
  45.8 0.0 copy-start.1
  45.8 0.0 copy-start.2
  45.8 3.5 %attend.1 = f32[16,8,512]{2,1,0:T(8,128)S(1)} custom-call(s32[1]{0:T(128)} %bitcast.core_ref, f32[16,2,8,384]{3,2,1,0:T(8,128)S(1)} %bitcast.6, f32[16,2,8,384]{3,2,1,0:T(8,128)S(1)} %bitcast.8, bf16[1152,384]{1,0:T(8,128)(2,1)S(1)} %get-tuple-element.22.wt_h, bf16[1152,384]{1,0:T(8,128)(2,1)S(1)} %get-tuple-element.23.wt_l, ...), custom_call_target="tpu_custom_call" | custom-call | flops 1000000000 | bytes 6291456 | tf_op jit(solution)/shard_map/attend/pallas_call | solution.py:260
  49.3 15.9 %all_to_all.10.parts = f32[16,8,512]{2,1,0:T(8,128)S(1)} all-to-all(f32[16,8,512]{2,1,0:T(8,128)S(1)} %attend.1), channel_id=1, replica_groups={{0,4,8,12,16,20,24,28,2,6,10,14,18,22,26,30},{1,5,9,13,17,21,25,29,3,7,..., dimensions={0} | all-to-all | bytes 524288 | tf_op jit(solution)/shard_map/all_to_all | solution.py:60
  65.2 0.0 copy-done
  65.2 0.0 copy-done.1
  65.2 0.0 copy-done.2
  65.2 1.0 %finish.1 = f32[8,384]{1,0:T(8,128)} custom-call(f32[16,8,512]{2,1,0:T(8,128)S(1)} %all_to_all.10.parts, f32[8,512]{1,0:T(8,128)S(1)} %get-tuple-element.24.gate, bf16[512,384]{1,0:T(8,128)(2,1)S(1)} %copy-done, bf16[512,384]{1,0:T(8,128)(2,1)S(1)} %copy-done.1, f32[8,384]{1,0:T(8,128)S(1)} %copy-done.2), custom_call_target="tpu_custom_call" | custom-call | flops 9437184 | bytes 2097152 | tf_op jit(solution)/shard_map/finish/pallas_call | solution.py:290
Async XLA Ops:
  0.0 12.7 %collective-permute-start.1 = (f32[8,384]{1,0:T(8,128)}, f32[8,384]{1,0:T(8,128)S(1)}, u32[]{:S(2)}, u32[]{:S(2)}) collective-permute-start(f32[8,384]{1,0:T(8,128)} %singles.2), channel_id=1, source_target_pairs={{1,129},{3,385},{5,97},{7,353},{9,65},{11,321},{13,33},{15,289},{1... | collective-permute-start | bytes 36872 | tf_op jit(solution)/shard_map/ppermute | solution.py:301
  8.3 9.1 %collective-permute-start = (f32[8,384]{1,0:T(8,128)}, f32[8,384]{1,0:T(8,128)S(1)}, u32[]{:S(2)}, u32[]{:S(2)}) collective-permute-start(f32[8,384]{1,0:T(8,128)} %singles.2), channel_id=1, source_target_pairs={{0,129},{2,385},{4,97},{6,353},{8,65},{10,321},{12,33},{14,289},{1... | collective-permute-start | bytes 36872 | tf_op jit(solution)/shard_map/ppermute | solution.py:302
  18.9 23.1 %all-to-all-start = ((f32[16,16,384]{2,1,0:T(8,128)}), f32[16,16,384]{2,1,0:T(8,128)S(1)}, u32[]{:S(2)}, u32[]{:S(2)}) async-start(f32[16,16,384]{2,1,0:T(8,128)} %broadcast_in_dim.2), calls=%async_computation | async-start | bytes 786432 | tf_op jit(solution)/shard_map/all_to_all | solution.py:60
  36.8 7.7 %collective-permute-start.3 = (f32[16,16,8,128]{3,2,1,0:T(8,128)}, f32[16,16,8,128]{3,2,1,0:T(8,128)S(1)}, u32[]{:S(2)}, u32[]{:S(2)}) collective-permute-start(f32[16,16,8,128]{3,2,1,0:T(8,128)} %cut.1), channel_id=1, source_target_pairs={{0,1},{1,0},{2,3},{3,2},{4,5},{5,4},{6,7},{7,6},{8,9},{9,8},{10,11... | collective-permute-start | bytes 3145736 | tf_op jit(solution)/shard_map/ppermute | solution.py:304
  42.0 3.7 %collective-permute-start.2 = (f32[16,16,384]{2,1,0:T(8,128)S(1)}, f32[16,16,384]{2,1,0:T(8,128)S(1)}, u32[]{:S(2)}, u32[]{:S(2)}) collective-permute-start(f32[16,16,384]{2,1,0:T(8,128)S(1)} %all-to-all-done), channel_id=1, source_target_pairs={{0,1},{1,0},{2,3},{3,2},{4,5},{5,4},{6,7},{7,6},{8,9},{9,8},{10,11... | collective-permute-start | bytes 1179656 | tf_op jit(solution)/shard_map/ppermute | solution.py:310
  45.8 19.4 %copy-start = (bf16[512,384]{1,0:T(8,128)(2,1)S(1)}, bf16[512,384]{1,0:T(8,128)(2,1)}, u32[]{:S(2)}) copy-start(bf16[512,384]{1,0:T(8,128)(2,1)} %get-tuple-element.25.wo_h) | copy-start | bytes 1179652
  45.8 19.4 %copy-start.1 = (bf16[512,384]{1,0:T(8,128)(2,1)S(1)}, bf16[512,384]{1,0:T(8,128)(2,1)}, u32[]{:S(2)}) copy-start(bf16[512,384]{1,0:T(8,128)(2,1)} %get-tuple-element.26.wo_l) | copy-start | bytes 1179652
  45.8 19.4 %copy-start.2 = (f32[8,384]{1,0:T(8,128)S(1)}, f32[8,384]{1,0:T(8,128)}, u32[]{:S(2)}) copy-start(f32[8,384]{1,0:T(8,128)} %singles.2) | copy-start | bytes 36868
